TPU v7x, 32 devices: a whole 2x2x4 slice. The times are simulated.
32 devices in a mesh: dp: 4 (over z), chan: 2 (over y), seq: 4 (over x, core).
Axes of the slice: x: 2, y: 2, z: 4, core: 2. Of those that a mesh axis runs over, the one named last changes fastest.
Arguments:
- tokens: bfloat16 [4, 4096, 768], P('dp', 'seq', 'chan'), may hold values from -6 to 6
- chan_in: bfloat16 [12, 64, 64], replicated, may hold values from -0.75 to 0.75
- chan_out: bfloat16 [64, 12, 12], replicated, may hold values from -1.75 to 1.75
- seq_in: bfloat16 [1024, 1024], replicated, may hold values from -0.1875 to 0.1875
- seq_out: bfloat16 [4, 4], replicated, may hold values from -3 to 3
- head_grad: bfloat16 [4, 4096, 768], P('dp', 'seq', 'chan'), may hold values from -6 to 6
- masked: int32 [4, 4096], P('dp', 'seq'), may hold values 0 or 1
Outputs:
- x_grad: bfloat16 [4, 4096, 768], P('dp', 'seq', 'chan')
- chan_in_grad: float32 [12, 64, 64], replicated
- chan_out_grad: float32 [64, 12, 12], replicated
- seq_in_grad: float32 [1024, 1024], P('seq')
- seq_out_grad: float32 [4, 4], replicated
All inputs are finite; a program needn't handle non-finite values. No bound on the sum of `masked` on one device may be relied on, other than what follows from the above.
Results may differ from a plain program's by a relative error of at most 0.0083.
Values may be sent and summed in bfloat16 or wider, within the bound.
No kernel may reach another device: no remote copies, remote signals or barrier semaphores. Data moves between devices by JAX's collectives and lax.ppermute only.
A program may use at most 64 MiB of HBM per device.

v0:
```python
import jax
import jax.numpy as jnp
from jax import lax
from jax.sharding import PartitionSpec as P


def silu_grad(values):
    sig = jax.nn.sigmoid(values)
    return sig * (1.0 + values * (1.0 - sig))


def per_device(tokens, chan_in, chan_out, seq_in, seq_out, head_grad, masked):
    chan_count = lax.axis_size("chan")
    seq_count = lax.axis_size("seq")
    chan_index = lax.axis_index("chan")
    seq_index = lax.axis_index("seq")
    sequences, positions, local_width = tokens.shape
    block_count = chan_in.shape[0]
    block_size = chan_in.shape[1]
    local_blocks = block_count // chan_count
    local_lanes = block_size // chan_count
    per_group = positions // seq_count
    in_blocks = lax.dynamic_slice_in_dim(chan_in, chan_index * local_blocks, local_blocks, 0)
    out_blocks = lax.dynamic_slice_in_dim(chan_out, chan_index * local_lanes, local_lanes, 0)
    features = tokens.reshape(sequences, positions, local_blocks, block_size)
    first_mix = jnp.einsum(
        "stbk,bki->stib", features, in_blocks, preferred_element_type=jnp.float32
    ).astype(jnp.bfloat16)
    turned = lax.all_to_all(first_mix, "chan", split_axis=2, concat_axis=3, tiled=True)
    channel_mix = jnp.einsum(
        "stib,ibe->stie", turned, out_blocks, preferred_element_type=jnp.float32
    ).astype(jnp.bfloat16)
    channel_mix = channel_mix.reshape(sequences, positions, local_width)
    row_mix = jnp.einsum(
        "stc,tr->src", channel_mix, seq_in, preferred_element_type=jnp.float32
    ).astype(jnp.bfloat16)
    row_blocks = row_mix.reshape(sequences, seq_count, per_group, local_width)
    spread = lax.all_to_all(row_blocks, "seq", split_axis=1, concat_axis=1, tiled=True)
    seq_mix = jnp.einsum("sagc,ab->sgbc", spread, seq_out, preferred_element_type=jnp.float32)
    seq_mix = seq_mix.reshape(sequences, positions, local_width)
    mix_float = channel_mix.astype(jnp.float32)
    upstream = masked[:, :, None].astype(jnp.float32) * head_grad.astype(jnp.float32)
    gated_grad = (upstream * jax.nn.silu(mix_float)).astype(jnp.bfloat16)
    gate_grad = upstream * seq_mix * silu_grad(mix_float)
    gated_blocks = gated_grad.reshape(sequences, per_group, seq_count, local_width)
    row_grad = jnp.einsum(
        "ab,sgbc->sagc", seq_out, gated_blocks, preferred_element_type=jnp.float32
    ).astype(jnp.bfloat16)
    second_local = jnp.einsum(
        "sagc,sgbc->ab", spread, gated_blocks, preferred_element_type=jnp.float32
    )
    returned_rows = lax.all_to_all(row_grad, "seq", split_axis=1, concat_axis=1, tiled=True)
    returned_rows = returned_rows.reshape(sequences, positions, local_width)
    seq_part = jnp.einsum("tr,src->stc", seq_in, returned_rows, preferred_element_type=jnp.float32)
    mix_grad = (gate_grad + seq_part).astype(jnp.bfloat16)
    mix_grad = mix_grad.reshape(sequences, positions, local_lanes, block_count)
    first_grad = jnp.einsum(
        "ibe,stie->stib", out_blocks, mix_grad, preferred_element_type=jnp.float32
    ).astype(jnp.bfloat16)
    out_local = jnp.einsum("stib,stie->ibe", turned, mix_grad, preferred_element_type=jnp.float32)
    owned_grad = lax.all_to_all(first_grad, "chan", split_axis=3, concat_axis=2, tiled=True)
    x_grad = jnp.einsum("bki,stib->stbk", in_blocks, owned_grad, preferred_element_type=jnp.float32)
    x_grad = x_grad.astype(jnp.bfloat16).reshape(sequences, positions, local_width)
    in_local = jnp.einsum(
        "stbk,stib->bki", features, owned_grad, preferred_element_type=jnp.float32
    )
    in_full = lax.dynamic_update_slice_in_dim(
        jnp.zeros((block_count, block_size, block_size), jnp.float32),
        in_local,
        chan_index * local_blocks,
        0,
    )
    out_full = lax.dynamic_update_slice_in_dim(
        jnp.zeros((block_size, block_count, block_count), jnp.float32),
        out_local,
        chan_index * local_lanes,
        0,
    )
    first_local = jnp.einsum(
        "stc,src->tr", channel_mix, returned_rows, preferred_element_type=jnp.float32
    )
    in_sum, out_sum, first_sum, second_sum = lax.psum(
        (in_full, out_full, first_local, second_local), ("dp", "chan", "seq")
    )
    first_rows = lax.dynamic_slice_in_dim(first_sum, seq_index * per_group, per_group, 0)
    return (x_grad, in_sum, out_sum, first_rows, second_sum)


def solution(mesh):
    in_specs = (P("dp", "seq", "chan"), P(), P(), P(), P(), P("dp", "seq", "chan"), P("dp", "seq"))
    out_specs = (P("dp", "seq", "chan"), P(), P(), P("seq", None), P())
    return jax.shard_map(
        per_device, mesh=mesh, in_specs=in_specs, out_specs=out_specs, check_vma=False
    )
```

profile of v0, /device:TPU:0, one launch (start us, length us, event | category | flops | bytes accessed | tf_op | source)
XLA Modules:
  0.0 251.9 jit_solution(14910816636616173630)
XLA Ops:
  7.2 1.6 copy.80
  9.3 1.4 copy.81
  10.7 4.2 %all-to-all-start = ((bf16[1,1024,64,6]{1,3,0,2:T(8,128)(2,1)}), bf16[1,1024,64,6]{1,3,0,2:T(8,128)(2,1)S(1)}, u32[]{:S(2)}, u32[]{:S(2)}) async-start(bf16[1,1024,64,6]{1,3,0,2:T(8,128)(2,1)} %copy.81), calls=%async_computation | async-start | bytes 2097152 | tf_op jit(solution)/shard_map/all_to_all | solution.py:29
  15.2 14.1 %all-to-all-done = bf16[1,1024,64,6]{1,3,0,2:T(8,128)(2,1)S(1)} async-done(((bf16[1,1024,64,6]{1,3,0,2:T(8,128)(2,1)}), bf16[1,1024,64,6]{1,3,0,2:T(8,128)(2,1)S(1)}, u32[]{:S(2)}, u32[]{:S(2)}) %all-to-all-start) | async-done | bytes 786464 | tf_op jit(solution)/shard_map/all_to_all | solution.py:29
  32.6 3.0 %fusion.4 = bf16[1024,384]{0,1:T(8,128)(2,1)} fusion(bf16[1024,384]{0,1:T(8,128)(2,1)} %reshape.152, bf16[1024,1024]{1,0:T(8,128)(2,1)S(1)} %copy-done), kind=kOutput, calls=%fused_computation.15 | convolution fusion | flops 805699584 | bytes 3670016 | tf_op jit(solution)/shard_map/stc,tr->src/dot_general | solution.py:34
  35.6 2.3 copy.105
  37.9 4.2 %all-to-all-start.1 = ((bf16[1,4,256,384]{3,2,0,1:T(8,128)(2,1)}), bf16[1,4,256,384]{3,2,0,1:T(8,128)(2,1)}, u32[]{:S(2)}, u32[]{:S(2)}) async-start(bf16[1,4,256,384]{3,2,0,1:T(8,128)(2,1)} %bitcast.93), calls=%async_computation.1 | async-start | bytes 1572864 | tf_op jit(solution)/shard_map/all_to_all | solution.py:38
  42.1 2.3 copy.77
  44.4 1.3 reshape.165
  45.7 3.0 %multiply_convert_fusion = bf16[1,1024,384]{1,2,0:T(8,128)(2,1)} fusion(f32[1,1024,384]{1,2,0:T(8,128)} %reshape.165, bf16[1,1024,384]{1,2,0:T(8,128)(2,1)} %copy.77, f32[1024]{0:T(1024)S(1)} %bitcast.95), kind=kLoop, calls=%fused_computation.2 | loop fusion | flops 3145728 | bytes 3149824 | tf_op jit(solution)/shard_map/convert_element_type | solution.py:43
  48.7 1.5 copy.92
  50.2 1.1 reshape.156
  51.3 1.7 fusion.5
  54.0 3.5 %all-to-all-start.2 = ((bf16[1,4,256,384]{3,2,0,1:T(8,128)(2,1)}), bf16[1,4,256,384]{3,2,0,1:T(8,128)(2,1)S(1)}, u32[]{:S(2)}, u32[]{:S(2)}) async-start(bf16[1,4,256,384]{3,2,0,1:T(8,128)(2,1)} %copy.93), calls=%async_computation.2 | async-start | bytes 1572864 | tf_op jit(solution)/shard_map/all_to_all | solution.py:52
  57.5 3.0 %convolution_bitcast_fusion = f32[1,256,4,384]{3,2,1,0:T(4,128)} fusion(bf16[1,4,256,384]{3,2,0,1:T(8,128)(2,1)} %all-to-all-done.1, bf16[4,4]{1,0:T(4,128)(2,1)S(1)} %copy-done.15), kind=kOutput, calls=%fused_computation.6 | convolution fusion | flops 3145728 | bytes 2359328 | tf_op jit(solution)/shard_map/sagc,ab->sgbc/dot_general | solution.py:39
  60.5 2.8 %reshape.155 = f32[1,1024,384]{2,1,0:T(8,128)} reshape(f32[1,256,4,384]{3,2,1,0:T(4,128)} %convolution_bitcast_fusion) | data formatting | bytes 3145728 | tf_op jit(solution)/shard_map/reshape | solution.py:40
  63.3 3.0 %copy.88 = f32[1,1024,384]{1,2,0:T(8,128)} copy(f32[1,1024,384]{2,1,0:T(8,128)} %reshape.155) | data formatting | bytes 3145728 | tf_op jit(solution)/shard_map/reshape | solution.py:40
  66.3 2.8 %all-to-all-done.2 = bf16[1,4,256,384]{3,2,0,1:T(8,128)(2,1)S(1)} async-done(((bf16[1,4,256,384]{3,2,0,1:T(8,128)(2,1)}), bf16[1,4,256,384]{3,2,0,1:T(8,128)(2,1)S(1)}, u32[]{:S(2)}, u32[]{:S(2)}) %all-to-all-start.2) | async-done | bytes 786464 | tf_op jit(solution)/shard_map/all_to_all | solution.py:52
  70.0 4.4 %fusion = bf16[1,1024,384]{1,2,0:T(8,128)(2,1)} fusion(f32[1,1024,384]{1,2,0:T(8,128)} %reshape.165, f32[1,1024,384]{1,2,0:T(8,128)} %copy.88, bf16[1,1024,384]{1,2,0:T(8,128)(2,1)} %copy.77, bf16[1024,384]{1,0:T(8,128)(2,1)S(1)} %bitcast.90, bf16[1024,1024]{1,0:T(8,128)(2,1)S(1)} %copy-done, f32[1024]{0:T(1024)S(1)} %bitcast.96), kind=kOutput, calls=%fused_computation.1 | convolution fusion | flops 810418176 | bytes 7606272 | tf_op jit(solution)/shard_map/tr,src->stc/dot_general | solution.py:54
  74.3 1.2 reshape.158
  77.1 1.3 copy.95
  78.4 4.3 %all-to-all-start.3 = ((bf16[1,1024,32,12]{1,2,0,3:T(8,128)(2,1)}), bf16[1,1024,32,12]{1,2,0,3:T(8,128)(2,1)}, u32[]{:S(2)}, u32[]{:S(2)}) async-start(bf16[1,1024,32,12]{1,2,0,3:T(8,128)(2,1)} %copy.95), calls=%async_computation.3 | async-start | bytes 1572864 | tf_op jit(solution)/shard_map/all_to_all | solution.py:61
  83.0 4.4 %fusion.19 = f32[1024,1024]{1,0:T(8,128)} fusion(bf16[1024,384]{0,1:T(8,128)(2,1)S(1)} %copy-done.5, bf16[1024,384]{1,0:T(8,128)(2,1)} %bitcast.91), kind=kOutput, calls=%fused_computation.35 | convolution fusion | flops 805306368 | bytes 5767168 | tf_op jit(solution)/shard_map/stc,src->tr/dot_general | solution.py:79
  87.4 6.3 %all-to-all-done.3 = bf16[1,1024,32,12]{1,2,0,3:T(8,128)(2,1)} async-done(((bf16[1,1024,32,12]{1,2,0,3:T(8,128)(2,1)}), bf16[1,1024,32,12]{1,2,0,3:T(8,128)(2,1)}, u32[]{:S(2)}, u32[]{:S(2)}) %all-to-all-start.3) | async-done | bytes 786464 | tf_op jit(solution)/shard_map/all_to_all | solution.py:61
  93.7 1.2 copy.96
  97.6 1.9 fusion.6
  100.0 2.8 %convolution_bitcast_fusion.2 = f32[4,4]{1,0:T(4,128)S(1)} fusion(bf16[256,4,384]{2,1,0:T(4,128)(2,1)} %reshape.156, bf16[1,4,256,384]{3,2,0,1:T(8,128)(2,1)} %all-to-all-done.1), kind=kOutput, calls=%fused_computation.18 | convolution fusion | flops 3145728 | bytes 1572928 | tf_op jit(solution)/shard_map/sagc,sgbc->ab/dot_general | solution.py:49
  102.8 41.9 %all-reduce = (f32[64,12,12]{0,2,1:T(8,128)}, f32[4,4]{1,0:T(4,128)}) all-reduce(f32[64,12,12]{0,2,1:T(8,128)S(1)} %dynamic_update_slice.7, f32[4,4]{1,0:T(4,128)S(1)} %convolution_bitcast_fusion.2), channel_id=1, replica_groups=mesh['dp'=4,'chan'=2,'seq'=4] {'dp','chan','seq'}, use_global_device_ids=true, to_apply=%region_1.2 | all-reduce | flops 9232 | bytes 73856 | tf_op jit(solution)/shard_map/psum | solution.py:82
  144.6 1.2 convolution_convert_fusion.3
  145.9 2.3 copy.101
  148.2 93.8 %all-reduce.4.cloned.1.call-done = (f32[12,64,64]{2,1,0:T(8,128)}, f32[1024,1024]{1,0:T(8,128)}) async-done(((f32[12,64,64]{2,1,0:T(8,128)}, f32[1024,1024]{1,0:T(8,128)}), (f32[12,64,64]{2,1,0:T(8,128)}, f32[1024,1024]{1,0:T(8,128)})) %all-reduce.4.cloned.1.call-update) | async-done | bytes 4390928 | tf_op jit(solution)/shard_map/psum | solution.py:82
  242.0 2.4 constant_dynamic-slice_fusion
  (53 shorter events, 11.5 us)
Async XLA Ops:
  7.2 25.4 %copy-start = (bf16[1024,1024]{1,0:T(8,128)(2,1)S(1)}, bf16[1024,1024]{1,0:T(8,128)(2,1)}, u32[]{:S(2)}) copy-start(bf16[1024,1024]{1,0:T(8,128)(2,1)} %param.10) | copy-start | bytes 6291460
  7.2 1.6 copy-start.12
  8.8 1.9 copy-start.1
  9.2 5.7 %copy-start.13 = (bf16[64,12,12]{0,2,1:T(8,128)(2,1)S(1)}, bf16[64,12,12]{0,2,1:T(8,128)(2,1)}, u32[]{:S(2)}) copy-start(bf16[64,12,12]{0,2,1:T(8,128)(2,1)} %param.9) | copy-start | bytes 55300
  10.7 18.7 %all-to-all-start = ((bf16[1,1024,64,6]{1,3,0,2:T(8,128)(2,1)}), bf16[1,1024,64,6]{1,3,0,2:T(8,128)(2,1)S(1)}, u32[]{:S(2)}, u32[]{:S(2)}) async-start(bf16[1,1024,64,6]{1,3,0,2:T(8,128)(2,1)} %copy.81), calls=%async_computation | async-start | bytes 2097152 | tf_op jit(solution)/shard_map/all_to_all | solution.py:29
  29.8 1.0 copy-start.6
  35.6 6.5 %copy-start.14 = (s32[1,1024]{1,0:T(1,128)S(1)}, s32[1,1024]{1,0:T(1,128)}, u32[]{:S(2)}) copy-start(s32[1,1024]{1,0:T(1,128)} %param.13) | copy-start | bytes 12292
  37.9 16.1 %all-to-all-start.1 = ((bf16[1,4,256,384]{3,2,0,1:T(8,128)(2,1)}), bf16[1,4,256,384]{3,2,0,1:T(8,128)(2,1)}, u32[]{:S(2)}, u32[]{:S(2)}) async-start(bf16[1,4,256,384]{3,2,0,1:T(8,128)(2,1)} %bitcast.93), calls=%async_computation.1 | async-start | bytes 1572864 | tf_op jit(solution)/shard_map/all_to_all | solution.py:38
  48.7 2.6 %copy-start.15 = (bf16[4,4]{1,0:T(4,128)(2,1)S(1)}, bf16[4,4]{1,0:T(4,128)(2,1)}, u32[]{:S(2)}) copy-start(bf16[4,4]{1,0:T(4,128)(2,1)} %param.11) | copy-start | bytes 100
  54.0 15.1 %all-to-all-start.2 = ((bf16[1,4,256,384]{3,2,0,1:T(8,128)(2,1)}), bf16[1,4,256,384]{3,2,0,1:T(8,128)(2,1)S(1)}, u32[]{:S(2)}, u32[]{:S(2)}) async-start(bf16[1,4,256,384]{3,2,0,1:T(8,128)(2,1)} %copy.93), calls=%async_computation.2 | async-start | bytes 1572864 | tf_op jit(solution)/shard_map/all_to_all | solution.py:52
  69.1 0.9 copy-start.9
  75.6 1.0 copy-start.8
  77.1 5.9 %copy-start.5 = (bf16[1024,384]{0,1:T(8,128)(2,1)S(1)}, bf16[1024,384]{0,1:T(8,128)(2,1)}, u32[]{:S(2)}) copy-start(bf16[1024,384]{0,1:T(8,128)(2,1)} %reshape.152) | copy-start | bytes 2359300
  78.4 15.3 %all-to-all-start.3 = ((bf16[1,1024,32,12]{1,2,0,3:T(8,128)(2,1)}), bf16[1,1024,32,12]{1,2,0,3:T(8,128)(2,1)}, u32[]{:S(2)}, u32[]{:S(2)}) async-start(bf16[1,1024,32,12]{1,2,0,3:T(8,128)(2,1)} %copy.95), calls=%async_computation.3 | async-start | bytes 1572864 | tf_op jit(solution)/shard_map/all_to_all | solution.py:61
  82.7 159.2 %all-reduce.4.cloned.1.call-start = ((), (), s32[]{:S(2)}) async-start(), calls=%async_computation.4 | async-start | bytes 9175040 | tf_op jit(solution)/shard_map/psum | solution.py:82
  87.4 8.4 %copy-start.2 = (bf16[1,1024,384]{1,2,0:T(8,128)(2,1)S(1)}, bf16[1,1024,384]{1,2,0:T(8,128)(2,1)}, u32[]{:S(2)}) copy-start(bf16[1,1024,384]{1,2,0:T(8,128)(2,1)} %copy-done.1) | copy-start | bytes 2359300
  94.9 0.9 copy-start.3
  96.3 0.7 copy-start.10
  96.3 1.3 copy-start.7
  100.0 44.6 %copy-start.4 = (bf16[1,1024,2,32,6]{1,3,2,4,0:T(8,128)(2,1)S(1)}, bf16[1,1024,2,32,6]{1,3,2,4,0:T(8,128)(2,1)}, u32[]{:S(2)}) copy-start(bf16[1,1024,2,32,6]{1,3,2,4,0:T(8,128)(2,1)} %copy-done.3) | copy-start | bytes 2359300
  242.0 2.4 copy-start.11
Sparse Core Ops, SparseCore 0:
  97.2 144.7 all-reduce.3
where the time goes:
time: 253 us; the launch traced here: 252 us
  waiting for transfers between devices  117 us (46%)
  blocking collectives  41.9 us (17%)
  local copies, waits for them, and re-layouts  35 us (14%)
  matrix products  24.3 us (10%)
  starting transfers between devices  16.5 us (7%)
  between operations  14.3 us (6%)
  other arithmetic  2.96 us (1%)
    psum x1, waiting for transfers between devices, per_device(): lax.psum((in_full, out_full, first_local, second_local), ('dp', 'chan', '...  93.8 us
    psum x1, blocking collectives, per_device(): lax.psum((in_full, out_full, first_local, second_local), ('dp', 'chan', '...  41.9 us
    all_to_all x1, waiting for transfers between devices, per_device(): lax.all_to_all(first_mix, 'chan', split_axis=2, concat_axis=3, tiled=True)  14.1 us
    unnamed x37, local copies, waits for them, and re-layouts  12.1 us
    all_to_all x1, waiting for transfers between devices, per_device(): lax.all_to_all(first_grad, 'chan', split_axis=3, concat_axis=2, tiled=True)  6.33 us
    reshape x2, local copies, waits for them, and re-layouts, per_device(): seq_mix = seq_mix.reshape(sequences, positions, local_width)  5.79 us
  transfers between devices with their start and end apart: 5, of which 4 were waited for; matrix products, arithmetic and copies ran while one was open for 14% of the time, Pallas kernels for 0%

commit v1 on v0

v1 whole, which is shorter than its diff:
```python
import functools

import jax
import jax.numpy as jnp
from jax import lax
from jax.experimental import pallas as pl
from jax.experimental.pallas import tpu as pltpu
from jax.sharding import PartitionSpec as P

F32 = jnp.float32
BF16 = jnp.bfloat16
VMEM_LIMIT = 48 * 1024 * 1024
PACK_LANES = 128


def dot(lhs, rhs, lhs_dim=1, rhs_dim=0):
    return lax.dot_general(
        lhs, rhs, (((lhs_dim,), (rhs_dim,)), ((), ())), preferred_element_type=F32
    )


def dot_exact(lhs, rhs, lhs_dim=1, rhs_dim=0):
    return lax.dot_general(
        lhs,
        rhs,
        (((lhs_dim,), (rhs_dim,)), ((), ())),
        precision=lax.Precision.HIGHEST,
        preferred_element_type=F32,
    )


def rows_of(shape):
    return lax.broadcasted_iota(jnp.int32, shape, 0)


def columns_of(shape):
    return lax.broadcasted_iota(jnp.int32, shape, 1)


def call(body, outs, args, scratch=(), flops=0, name=None):
    nbytes = sum(a.size * a.dtype.itemsize for a in list(args) + list(outs))
    return pl.pallas_call(
        body,
        out_shape=tuple(outs),
        in_specs=[pl.BlockSpec(memory_space=pltpu.VMEM)] * len(args),
        out_specs=tuple([pl.BlockSpec(memory_space=pltpu.VMEM)] * len(outs)),
        scratch_shapes=list(scratch),
        compiler_params=pltpu.CompilerParams(vmem_limit_bytes=VMEM_LIMIT),
        cost_estimate=pl.CostEstimate(flops=flops, bytes_accessed=nbytes, transcendentals=0),
        name=name,
    )(*args)


def struct(shape, dtype=BF16):
    return jax.ShapeDtypeStruct(shape, dtype)


class Sizes:
    def __init__(self, tokens, chan_in, seq_count):
        self.positions, self.width = tokens.shape
        self.blocks, self.block = chan_in.shape[0], chan_in.shape[1]
        self.my_blocks = self.blocks // 2
        self.my_lanes = self.block // 2
        self.half = self.positions // 2
        self.part = self.my_blocks * self.my_lanes
        self.seq = seq_count
        self.group = self.positions // seq_count
        self.step = min(64, self.group)
        self.chunk = self.step * seq_count
        self.chunks = self.positions // self.chunk
        self.direct = seq_count == 4


def in_matrices(z, blocks, lane_base):
    shape = (z.width, 2 * z.part)
    column = columns_of((z.block, 2 * z.part))
    pick = rows_of((z.block, 2 * z.part)) == lane_base + (column & (z.my_lanes - 1))
    spread = dot(blocks, pick.astype(BF16))
    row, column = rows_of(shape), columns_of(shape)
    left = column < z.part
    place = jnp.where(left, column, column - z.part)
    same = (row // z.block) == (place // z.my_lanes)
    lower = jnp.where(same & left, spread, 0.0).astype(BF16)
    upper = jnp.where(same & jnp.logical_not(left), spread, 0.0).astype(BF16)
    return lower, upper


def lane_masks(z):
    shape = (z.width, 2 * z.part)
    row, column = rows_of(shape), columns_of(shape)
    left = column < z.part
    place = jnp.where(left, column, column - z.part)
    same = (row // z.block) == (place // z.my_lanes)
    return same & left, same & jnp.logical_not(left)


def lane_of_channel(z, shape, axis):
    index = lax.broadcasted_iota(jnp.int32, shape, axis)
    lane = (index * 5462) >> 16
    return lane, index - z.blocks * lane


def out_mask(z):
    shape = (z.blocks * z.my_lanes, z.width)
    lane, _ = lane_of_channel(z, shape, 1)
    return (rows_of(shape) & (z.my_lanes - 1)) == lane


def out_matrix(z, factors):
    shape = (z.blocks, z.width)
    _, entry = lane_of_channel(z, shape, 1)
    spread = dot(factors, (rows_of(shape) == entry).astype(BF16))
    return jnp.where(out_mask(z), spread, 0.0).astype(BF16)


def position_masks(z):
    shape = (z.chunk, z.chunk)
    row, column = rows_of(shape), columns_of(shape)
    same = (row & (z.step - 1)) == (column // z.seq)
    blocks = (z.chunk, z.seq)
    of_a = (rows_of(blocks) // z.step) == columns_of(blocks)
    turned = (z.seq, z.chunk)
    of_a2 = (columns_of(turned) & (z.seq - 1)) == rows_of(turned)
    return same, of_a, of_a2


def position_matrix(z, factor):
    same, of_a, of_a2 = position_masks(z)
    by_row = dot(of_a.astype(BF16), factor).astype(BF16)
    return jnp.where(same, dot(by_row, of_a2.astype(BF16)), 0.0).astype(BF16)


def fill_padded(z, pad_ref, rows):
    zeros = jnp.zeros((z.part, z.width), BF16)
    pad_ref[0 : z.part, :] = zeros
    pad_ref[z.part : 2 * z.part, :] = rows
    pad_ref[2 * z.part : 3 * z.part, :] = zeros


def split_blocks(z, full_ref, refs):
    if not z.direct:
        refs[0][...] = full_ref[...]
        return
    mine = lax.axis_index("seq")
    for step, ref in enumerate(refs):
        ref[...] = full_ref[mine ^ step]


def join_blocks(z, refs, full_ref):
    if not z.direct:
        full_ref[...] = refs[0][...]
        return
    mine = lax.axis_index("seq")
    for step, ref in enumerate(refs):
        full_ref[mine ^ step] = ref[...]


def block_outs(z):
    if not z.direct:
        return [struct((z.seq, z.group, z.width))]
    return [struct((z.group, z.width))] * z.seq


def swap(value, axis, step):
    size = lax.axis_size(axis)
    return lax.ppermute(value, axis, [(i, i ^ step) for i in range(size)])


def exchange_blocks(z, blocks):
    if not z.direct:
        return [lax.all_to_all(blocks[0], "seq", split_axis=0, concat_axis=0, tiled=True)]
    return [blocks[0]] + [swap(blocks[step], "seq", step) for step in range(1, z.seq)]


def first_mix_kernel(z, x_ref, in_ref, own_ref, other_ref):
    chan = lax.axis_index("chan")
    blocks = in_ref[pl.ds(chan * z.my_blocks, z.my_blocks)].reshape(z.width, z.block)
    low, high = x_ref[: z.half, :], x_ref[z.half :, :]
    for base, ref in ((1 - chan, other_ref), (chan, own_ref)):
        lower, upper = in_matrices(z, blocks, base * z.my_lanes)
        ref[...] = (dot(low, lower) + dot(high, upper)).astype(BF16)


def prepare_kernel(z, head_ref, mask_ref, seq_ref, out_ref, up_ref, turn_ref, dense_ref):
    lines = jnp.broadcast_to(mask_ref[...].astype(F32), (16, z.positions)).astype(BF16)
    ones = jnp.full((16, z.width), 1.0 / 16.0, BF16)
    mask = dot(lines, ones, 0, 0)
    up_ref[...] = (mask * head_ref[...].astype(F32)).astype(BF16)
    turn_ref[...] = jnp.transpose(seq_ref[...])
    dense_ref[...] = out_matrix(z, out_ref[...])


def channel_mix_kernel(z, own_ref, got_ref, dense_ref, up_ref, so_ref, *rest):
    mix_ref, gated_ref = rest[:2]
    refs, (pad_ref, rows_ref) = rest[2:-2], rest[-2:]
    chan = lax.axis_index("chan")
    low = high = None
    for base, ref in ((chan, own_ref), (1 - chan, got_ref)):
        start = pl.multiple_of(base * z.part, z.part)
        fill_padded(z, pad_ref, dense_ref[pl.ds(start, z.part), :])
        first = dot(ref[...], pad_ref[z.part :, :])
        second = dot(ref[...], pad_ref[: 2 * z.part, :])
        low = first if low is None else low + first
        high = second if high is None else high + second
    for at, values in ((0, low), (z.half, high)):
        rounded = values.astype(BF16)
        mix_ref[at : at + z.half, :] = rounded
        mixed = rounded.astype(F32)
        upstream = up_ref[at : at + z.half, :].astype(F32)
        gated_ref[at : at + z.half, :] = (upstream * (mixed * jax.nn.sigmoid(mixed))).astype(BF16)
    matrix = position_matrix(z, so_ref[...])
    for j in range(z.chunks):
        out = dot(matrix, gated_ref[j * z.chunk : (j + 1) * z.chunk, :]).astype(BF16)
        rows_ref[:, j * z.step : (j + 1) * z.step, :] = out.reshape(z.seq, z.step, z.width)
    split_blocks(z, rows_ref, refs)


def row_mix_kernel(z, turn_ref, mix_ref, *rest):
    refs, rows_ref = rest[:-1], rest[-1]
    out = dot(turn_ref[...], mix_ref[...]).astype(BF16)
    rows_ref[...] = out.reshape(z.seq, z.group, z.width)
    split_blocks(z, rows_ref, refs)


def gate_kernel(z, mix_ref, up_ref, gate_ref):
    mixed = mix_ref[...].astype(F32)
    sig = jax.nn.sigmoid(mixed)
    gate_ref[...] = up_ref[...].astype(F32) * (sig * (1.0 + mixed * (1.0 - sig)))


def seq_grad_kernel(z, count, *rest):
    seq_ref, mix_ref = rest[:2]
    refs = rest[2 : 2 + count]
    part_ref = rest[2 + count]
    outs, rows_ref = rest[3 + count : -1], rest[-1]
    join_blocks(z, refs, rows_ref)
    rows = rows_ref[...].reshape(z.positions, z.width)
    part_ref[...] = dot(seq_ref[...], rows)
    if not z.direct:
        outs[0][...] = dot(mix_ref[...], rows, 1, 1)
        return
    mine = lax.axis_index("seq")
    core = mine & 1
    for x in range(2):
        for keep, out in ((core, outs[0]), (1 - core, outs[1])):
            start = pl.multiple_of((2 * x + keep) * z.group, z.group)
            out[x] = dot(mix_ref[pl.ds(start, z.group), :], rows, 1, 1).astype(BF16)


def mix_grad_kernel(z, count, *rest):
    gate_ref, part_ref, dense_ref, so_ref = rest[:4]
    refs = rest[4 : 4 + count]
    mixg_ref, own_ref, other_ref, spread_ref, pad_ref = rest[4 + count :]
    join_blocks(z, refs, spread_ref)
    matrix = position_matrix(z, so_ref[...])
    for j in range(z.chunks):
        rows = spread_ref[:, j * z.step : (j + 1) * z.step, :].reshape(z.chunk, z.width)
        seq_mix = dot(matrix, rows, 0, 0)
        at = slice(j * z.chunk, (j + 1) * z.chunk)
        mixg_ref[at, :] = (gate_ref[at, :] * seq_mix + part_ref[at, :]).astype(BF16)
    chan = lax.axis_index("chan")
    low, high = mixg_ref[: z.half, :], mixg_ref[z.half :, :]
    for base, ref in ((1 - chan, other_ref), (chan, own_ref)):
        start = pl.multiple_of(base * z.part, z.part)
        fill_padded(z, pad_ref, dense_ref[pl.ds(start, z.part), :])
        total = dot(low, pad_ref[z.part :, :], 1, 1) + dot(high, pad_ref[: 2 * z.part, :], 1, 1)
        ref[...] = total.astype(BF16)


def out_grad_kernel(z, count, *rest):
    own_ref, got_ref, mixg_ref, gated_ref = rest[:4]
    refs = rest[4 : 4 + count]
    out_ref, second_ref, spread_ref, full_ref = rest[4 + count :]
    join_blocks(z, refs, spread_ref)
    chan = lax.axis_index("chan")
    low, high = mixg_ref[: z.half, :], mixg_ref[z.half :, :]
    for base, ref in ((chan, own_ref), (1 - chan, got_ref)):
        first = dot(ref[...], low, 0, 0)[: z.part, :]
        second = dot(ref[...], high, 0, 0)[z.part :, :]
        full_ref[pl.ds(pl.multiple_of(base * z.part, z.part), z.part), :] = first + second
    kept = jnp.where(out_mask(z), full_ref[...], 0.0)
    shape = (z.width, PACK_LANES)
    _, entry = lane_of_channel(z, shape, 0)
    out_ref[...] = dot_exact(kept, (columns_of(shape) == z.block + entry).astype(F32))
    same, of_a, of_a2 = position_masks(z)
    total = jnp.zeros((z.chunk, z.chunk), F32)
    for j in range(z.chunks):
        rows = spread_ref[:, j * z.step : (j + 1) * z.step, :].reshape(z.chunk, z.width)
        total = total + dot(rows, gated_ref[j * z.chunk : (j + 1) * z.chunk, :], 1, 1)
    total = jnp.where(same, total, 0.0)
    shape = (z.chunk, PACK_LANES)
    to_a2 = ((rows_of(shape) & (z.seq - 1)) == columns_of(shape)).astype(F32)
    tall = (max(16, z.seq), z.chunk)
    to_a = ((columns_of(tall) // z.step) == rows_of(tall)).astype(F32)
    second_ref[...] = dot_exact(to_a, dot_exact(total, to_a2))


def in_grad_kernel(z, x_ref, in_ref, own_ref, got_ref, out_ref, second_ref, xg_ref, pack_ref):
    chan = lax.axis_index("chan")
    blocks = in_ref[pl.ds(chan * z.my_blocks, z.my_blocks)].reshape(z.width, z.block)
    low, high = x_ref[: z.half, :], x_ref[z.half :, :]
    left, right = lane_masks(z)
    shape = (2 * z.part, PACK_LANES)
    xg_low = xg_high = None
    pack = out_ref[...]
    for base, ref in ((chan, own_ref), (1 - chan, got_ref)):
        grad = ref[...]
        lower, upper = in_matrices(z, blocks, base * z.my_lanes)
        first, second = dot(grad, lower, 1, 1), dot(grad, upper, 1, 1)
        xg_low = first if xg_low is None else xg_low + first
        xg_high = second if xg_high is None else xg_high + second
        products = jnp.where(left, dot(low, grad, 0, 0), jnp.where(right, dot(high, grad, 0, 0), 0.0))
        lane = base * z.my_lanes + (rows_of(shape) & (z.my_lanes - 1))
        pack = pack + dot_exact(products, (columns_of(shape) == lane).astype(F32))
    xg_ref[: z.half, :] = xg_low.astype(BF16)
    xg_ref[z.half :, :] = xg_high.astype(BF16)
    pack_ref[: z.width, :] = pack.astype(BF16)
    pack_ref[z.width :, :] = second_ref[...].astype(BF16)


def sum_pairs(parts):
    parts = [part.astype(F32) for part in parts]
    while len(parts) > 1:
        parts = [parts[i] + parts[i + 1] for i in range(0, len(parts), 2)]
    return parts[0]


def sum_over(value, axis):
    size = lax.axis_size(axis)
    if size > 4:
        return lax.psum(value.astype(F32), axis)
    return sum_pairs([value] + [swap(value, axis, step) for step in range(1, size)])


def core_sum_kernel(keep_ref, got_ref, mine_ref, send_ref):
    x = lax.axis_index("seq") >> 1
    mine_ref[...] = keep_ref[x].astype(F32) + got_ref[x].astype(F32)
    send_ref[...] = (keep_ref[1 - x].astype(F32) + got_ref[1 - x].astype(F32)).astype(BF16)


def x_sum_kernel(keep_ref, got_ref, mine_ref, send_ref):
    chan = lax.axis_index("chan")
    rows = mine_ref.shape[0]
    for base, out in ((chan, mine_ref), (1 - chan, send_ref)):
        at = pl.ds(pl.multiple_of(base * rows, rows), rows)
        out[...] = (keep_ref[at, :] + got_ref[at, :].astype(F32)).astype(out.dtype)


def y_sum_kernel(keep_ref, got_ref, *outs):
    rows = outs[0].shape[0]
    dp = lax.axis_index("dp")
    for step, out in enumerate(outs):
        at = pl.ds(pl.multiple_of((dp ^ step) * rows, rows), rows)
        out[...] = (keep_ref[at, :] + got_ref[at, :].astype(F32)).astype(BF16)


def z_sum_kernel(own_ref, a_ref, b_ref, c_ref, out_ref):
    parts = [ref[...].astype(F32) for ref in (own_ref, a_ref, b_ref, c_ref)]
    out_ref[...] = ((parts[0] + parts[1]) + (parts[2] + parts[3])).astype(BF16)


def z_join_kernel(own_ref, a_ref, b_ref, c_ref, out_ref):
    rows = own_ref.shape[0]
    dp = lax.axis_index("dp")
    for step, ref in enumerate((own_ref, a_ref, b_ref, c_ref)):
        out_ref[pl.ds(pl.multiple_of((dp ^ step) * rows, rows), rows), :] = ref[...]


def y_join_kernel(own_ref, got_ref, out_ref):
    rows = own_ref.shape[0]
    chan = lax.axis_index("chan")
    for base, ref in ((chan, own_ref), (1 - chan, got_ref)):
        out_ref[pl.ds(pl.multiple_of(base * rows, rows), rows), :] = ref[...].astype(F32)


def sum_first(keep, send):
    _, rows, width = keep.shape
    got = swap(send, "seq", 1)
    mine, send = call(
        core_sum_kernel, [struct((rows, width), F32), struct((rows, width))], [keep, got], name="core_sum"
    )
    got = swap(send, "seq", 2)
    rows //= 2
    mine, send = call(
        x_sum_kernel, [struct((rows, width), F32), struct((rows, width))], [mine, got], name="x_sum"
    )
    got = swap(send, "chan", 1)
    rows //= 4
    parts = call(y_sum_kernel, [struct((rows, width))] * 4, [mine, got], name="y_sum")
    parts = [parts[0]] + [swap(parts[step], "dp", step) for step in range(1, 4)]
    (own,) = call(z_sum_kernel, [struct((rows, width))], parts, name="z_sum")
    parts = [own] + [swap(own, "dp", step) for step in range(1, 4)]
    rows *= 4
    (own,) = call(z_join_kernel, [struct((rows, width))], parts, name="z_join")
    got = swap(own, "chan", 1)
    (full,) = call(y_join_kernel, [struct((2 * rows, width), F32)], [own, got], name="y_join")
    return full


def per_device(tokens, chan_in, chan_out, seq_in, seq_out, head_grad, masked):
    seq_count = lax.axis_size("seq")
    chan_index = lax.axis_index("chan")
    tokens, head_grad = tokens[0], head_grad[0]
    z = Sizes(tokens, chan_in, seq_count)
    wide = (z.positions, z.width)
    packed = (z.half, 2 * z.part)
    bind = functools.partial
    macs = 2 * z.positions * z.width

    own, other = call(
        bind(first_mix_kernel, z), [struct(packed)] * 2, [tokens, chan_in], flops=macs * 768, name="first_mix"
    )
    got = swap(other, "chan", 1)

    factors = lax.dynamic_slice_in_dim(chan_out, chan_index * z.my_lanes, z.my_lanes, 0)
    factors = jnp.transpose(factors, (1, 0, 2)).reshape(z.blocks * z.my_lanes, z.blocks)
    upstream, turned, dense = call(
        bind(prepare_kernel, z),
        [struct(wide), struct(seq_in.shape), struct((z.blocks * z.my_lanes, z.width))],
        [head_grad, masked, seq_in, factors],
        flops=macs * 64,
        name="prepare",
    )
    rows_scratch = pltpu.VMEM((z.seq, z.group, z.width), BF16)
    pad_scratch = pltpu.VMEM((3 * z.part, z.width), BF16)
    outs = call(
        bind(channel_mix_kernel, z),
        [struct(wide)] * 2 + block_outs(z),
        [own, got, dense, upstream, seq_out],
        [pad_scratch, rows_scratch],
        flops=macs * 1024,
        name="channel_mix",
    )
    mix, gated, row_grad = outs[0], outs[1], outs[2:]
    row_grad = exchange_blocks(z, row_grad)
    row_mix = call(
        bind(row_mix_kernel, z), block_outs(z), [turned, mix], [rows_scratch], flops=macs * 1024, name="row_mix"
    )
    spread = exchange_blocks(z, row_mix)
    (gate,) = call(bind(gate_kernel, z), [struct(wide, F32)], [mix, upstream], flops=macs * 64, name="gate")
    count = len(row_grad)
    if z.direct:
        outs = [struct((2, z.group, seq_in.shape[1]))] * 2
    else:
        outs = [struct(seq_in.shape, F32)]
    seq_part, *first_parts = call(
        bind(seq_grad_kernel, z, count),
        [struct(wide, F32)] + outs,
        [seq_in, mix] + list(row_grad),
        [rows_scratch],
        flops=macs * 2048,
        name="seq_grad",
    )
    mix_grad, own_grad, other_grad = call(
        bind(mix_grad_kernel, z, count),
        [struct(wide)] + [struct(packed)] * 2,
        [gate, seq_part, dense, seq_out] + list(spread),
        [rows_scratch, pad_scratch],
        flops=macs * 1024,
        name="mix_grad",
    )
    got_grad = swap(other_grad, "chan", 1)
    out_part, second_part = call(
        bind(out_grad_kernel, z, count),
        [struct((z.width, PACK_LANES), F32), struct((max(16, z.seq), PACK_LANES), F32)],
        [own, got, mix_grad, gated] + list(spread),
        [rows_scratch, pltpu.VMEM((2 * z.part, z.width), F32)],
        flops=macs * 1024,
        name="out_grad",
    )
    x_grad, pack = call(
        bind(in_grad_kernel, z),
        [struct(wide), struct((z.width + second_part.shape[0], PACK_LANES))],
        [tokens, chan_in, own_grad, got_grad, out_part, second_part],
        flops=macs * 1536,
        name="in_grad",
    )
    if z.direct:
        first_rows = sum_first(*first_parts)
    else:
        first_rows = lax.psum_scatter(first_parts[0], "seq", scatter_dimension=0, tiled=True)
        first_rows = lax.psum(first_rows, ("dp", "chan"))
    pack = sum_over(pack, "seq").astype(BF16)
    pack = sum_over(pack, "dp").astype(BF16)
    there = swap(pack, "chan", 1)
    both = jnp.stack([jnp.where(chan_index == 0, pack, there), jnp.where(chan_index == 0, there, pack)])
    both = both.astype(F32)
    in_sum = both[:, : z.width, : z.block].reshape(z.blocks, z.block, z.block)
    out_sum = both[:, : z.width, z.block : z.block + z.blocks]
    out_sum = out_sum.reshape(2, z.blocks, z.my_lanes, z.blocks)
    out_sum = jnp.transpose(out_sum, (0, 2, 1, 3)).reshape(z.block, z.blocks, z.blocks)
    second_sum = both[0, z.width : z.width + z.seq, : z.seq] + both[1, z.width : z.width + z.seq, : z.seq]
    return (x_grad[None], in_sum, out_sum, first_rows, second_sum)


def solution(mesh):
    in_specs = (P("dp", "seq", "chan"), P(), P(), P(), P(), P("dp", "seq", "chan"), P("dp", "seq"))
    out_specs = (P("dp", "seq", "chan"), P(), P(), P("seq", None), P())
    return jax.shard_map(
        per_device, mesh=mesh, in_specs=in_specs, out_specs=out_specs, check_vma=False
    )
```

time: 253 us -> 104 us (0.41)
  waiting for transfers between devices: 117 us -> 43.9 us
  blocking collectives: 41.9 us -> 0 us
  local copies, waits for them, and re-layouts: 35 us -> 5.55 us
  matrix products: 24.3 us -> 0 us
  Pallas kernels: 0 us -> 19.6 us
  starting transfers between devices: 16.5 us -> 33.4 us
  between operations: 14.3 us -> 0.85 us
    psum x1 -> x0, waiting for transfers between devices: 93.8 us -> none  [per_device(): lax.psum((in_full, out_full, first_local, second_local), ('dp', 'chan', '...]
    ppermute x0 -> x25, waiting for transfers between devices: none -> 43.9 us  [swap(): return lax.ppermute(value, axis, [(i, i ^ step) for i in range(size)])]
    psum x1 -> x0, blocking collectives: 41.9 us -> none  [per_device(): lax.psum((in_full, out_full, first_local, second_local), ('dp', 'chan', '...]
    ppermute x0 -> x25, starting transfers between devices: none -> 33.4 us  [swap(): return lax.ppermute(value, axis, [(i, i ^ step) for i in range(size)])]
    dot_general x12 -> x0, matrix products: 24.3 us -> none  [the longest x1 4.39 us: per_device(): jnp.einsum('stc,src->tr', channel_mix, returned_rows, preferred_element_t...]
    all_to_all x4 -> x0, waiting for transfers between devices: 23.2 us -> none  [the longest x1 14.1 us: per_device(): lax.all_to_all(first_mix, 'chan', split_axis=2, concat_axis=3, tiled=True)]
    pallas_call x0 -> x15, Pallas kernels: none -> 19.6 us  [call(): pl.pallas_call(body, out_shape=tuple(outs), in_specs=[pl.BlockSpec(memory...]
    all_to_all x4 -> x0, starting transfers between devices: 16.2 us -> none  [the longest x1 4.33 us: per_device(): lax.all_to_all(first_grad, 'chan', split_axis=3, concat_axis=2, tiled=True)]
  transfers between devices with their start and end apart: 5 -> 25, of which waited for: 4 -> 12; matrix products, arithmetic and copies ran while one was open for 14% -> 3% of each run, Pallas kernels for 0% -> 11%
where the time goes in v1:
time: 104 us
  waiting for transfers between devices  43.9 us (42%)
  starting transfers between devices  33.4 us (32%)
  Pallas kernels  19.6 us (19%)
  local copies, waits for them, and re-layouts  5.55 us (5%)
    ppermute x25, waiting for transfers between devices, swap(): return lax.ppermute(value, axis, [(i, i ^ step) for i in range(size)])  43.9 us
    ppermute x25, starting transfers between devices, swap(): return lax.ppermute(value, axis, [(i, i ^ step) for i in range(size)])  33.4 us
    pallas_call x15, Pallas kernels, call(): pl.pallas_call(body, out_shape=tuple(outs), in_specs=[pl.BlockSpec(memory...  19.6 us
    unnamed x18, local copies, waits for them, and re-layouts  3.37 us
  transfers between devices with their start and end apart: 25, of which 12 were waited for; matrix products, arithmetic and copies ran while one was open for 3% of the time, Pallas kernels for 11%

profile of v1, /device:TPU:0, one launch (start us, length us, event | category | flops | bytes accessed | tf_op | source)
XLA Modules:
  0.0 104.0 jit_solution(845091988140771119)
XLA Ops:
  2.9 1.5 %first_mix.1 = (bf16[512,384]{1,0:T(8,128)(2,1)S(1)}, bf16[512,384]{1,0:T(8,128)(2,1)S(1)}) custom-call(bf16[1024,384]{1,0:T(8,128)(2,1)S(1)} %bitcast.20, bf16[12,64,64]{2,1,0:T(8,128)(2,1)S(1)} %copy-done.7), custom_call_target="tpu_custom_call" | custom-call | flops 603979776 | bytes 1671168 | tf_op jit(solution)/shard_map/first_mix/pallas_call | solution.py:42
  4.4 3.0 %collective-permute-start = (bf16[512,384]{1,0:T(8,128)(2,1)S(1)}, bf16[512,384]{1,0:T(8,128)(2,1)S(1)}, u32[]{:S(2)}, u32[]{:S(2)}) collective-permute-start(bf16[512,384]{1,0:T(8,128)(2,1)S(1)} %get-tuple-element.39), channel_id=1, source_target_pairs={{0,4},{4,0},{1,5},{5,1},{2,6},{6,2},{3,7},{7,3},{8,12},{12,8},{9,1... | collective-permute-start | bytes 1179656 | tf_op jit(solution)/shard_map/ppermute | solution.py:166
  9.6 6.9 %collective-permute-done.got_ref.rest_1_ = bf16[512,384]{1,0:T(8,128)(2,1)S(1)} collective-permute-done((bf16[512,384]{1,0:T(8,128)(2,1)S(1)}, bf16[512,384]{1,0:T(8,128)(2,1)S(1)}, u32[]{:S(2)}, u32[]{:S(2)}) %collective-permute-start) | collective-permute-done | bytes 393248 | tf_op jit(solution)/shard_map/ppermute | solution.py:166
  16.5 2.0 %channel_mix.1 = (bf16[1024,384]{1,0:T(8,128)(2,1)S(1)}, bf16[1024,384]{1,0:T(8,128)(2,1)S(1)}, bf16[256,384]{1,0:T(8,128)(2,1)S(1)}, bf16[256,384]{1,0:T(8,128)...) custom-call(bf16[512,384]{1,0:T(8,128)(2,1)S(1)} %get-tuple-element.38.own_ref.rest_0_, ...), custom_call_target="tpu_custom_call" | custom-call | flops 805306368 | bytes 4227104 | tf_op jit(solution)/shard_map/channel_mix/pallas_call | solution.py:42
  18.6 1.8 %collective-permute-start.2 = (bf16[256,384]{1,0:T(8,128)(2,1)S(1)}, bf16[256,384]{1,0:T(8,128)(2,1)S(1)}, u32[]{:S(2)}, u32[]{:S(2)}) collective-permute-start(bf16[256,384]{1,0:T(8,128)(2,1)S(1)} %get-tuple-element.45), channel_id=1, source_target_pairs={{0,2},{1,3},{2,0},{3,1},{4,6},{5,7},{6,4},{7,5},{8,10},{9,11},{10,... | collective-permute-start | bytes 589832 | tf_op jit(solution)/shard_map/ppermute | solution.py:166
  20.5 5.9 %collective-permute-done.2.rest_4_ = bf16[256,384]{1,0:T(8,128)(2,1)S(1)} collective-permute-done((bf16[256,384]{1,0:T(8,128)(2,1)S(1)}, bf16[256,384]{1,0:T(8,128)(2,1)S(1)}, u32[]{:S(2)}, u32[]{:S(2)}) %collective-permute-start.2) | collective-permute-done | bytes 196640 | tf_op jit(solution)/shard_map/ppermute | solution.py:166
  26.4 3.3 %collective-permute-done.3.rest_5_ = bf16[256,384]{1,0:T(8,128)(2,1)S(1)} collective-permute-done((bf16[256,384]{1,0:T(8,128)(2,1)S(1)}, bf16[256,384]{1,0:T(8,128)(2,1)S(1)}, u32[]{:S(2)}, u32[]{:S(2)}) %collective-permute-start.3) | collective-permute-done | bytes 196640 | tf_op jit(solution)/shard_map/ppermute | solution.py:166
  29.7 4.0 %seq_grad.1 = (f32[1024,384]{1,0:T(8,128)S(1)}, bf16[2,256,1024]{2,1,0:T(8,128)(2,1)S(1)}, bf16[2,256,1024]{2,1,0:T(8,128)(2,1)S(1)}) custom-call(bf16[1024,1024]{1,0:T(8,128)(2,1)} %rest_0_.1, bf16[1024,384]{1,0:T(8,128)(2,1)S(1)} %get-tuple-element.42.mix_ref.rest_1_, bf16[256,384]{1,0:T(8,128)(2,1)S(1)} %get-tuple-element.43.rest_2_, ...), custom_call_target="tpu_custom_call" | custom-call | flops 1610612736 | bytes 7340032 | tf_op jit(solution)/shard_map/seq_grad/pallas_call | solution.py:42
  34.1 1.3 %row_mix.1 = (bf16[256,384]{1,0:T(8,128)(2,1)S(1)}, bf16[256,384]{1,0:T(8,128)(2,1)S(1)}, bf16[256,384]{1,0:T(8,128)(2,1)S(1)}, bf16[256,384]{1,0:T(8,128)(2,1)S(1)}) custom-call(bf16[1024,1024]{1,0:T(8,128)(2,1)S(1)} %get-tuple-element.48.turn_ref, bf16[1024,384]{1,0:T(8,128)(2,1)S(1)} %get-tuple-element.42.mix_ref.rest_1_), custom_call_target="tpu_custom_call" | custom-call | flops 805306368 | bytes 3670016 | tf_op jit(solution)/shard_map/row_mix/pallas_call | solution.py:42
  35.7 1.7 %collective-permute-start.5 = (bf16[256,384]{1,0:T(8,128)(2,1)S(1)}, bf16[256,384]{1,0:T(8,128)(2,1)S(1)}, u32[]{:S(2)}, u32[]{:S(2)}) collective-permute-start(bf16[256,384]{1,0:T(8,128)(2,1)S(1)} %get-tuple-element.51), channel_id=1, source_target_pairs={{0,2},{1,3},{2,0},{3,1},{4,6},{5,7},{6,4},{7,5},{8,10},{9,11},{10,... | collective-permute-start | bytes 589832 | tf_op jit(solution)/shard_map/ppermute | solution.py:166
  38.0 5.5 %collective-permute-done.5.rest_6_ = bf16[256,384]{1,0:T(8,128)(2,1)S(1)} collective-permute-done((bf16[256,384]{1,0:T(8,128)(2,1)S(1)}, bf16[256,384]{1,0:T(8,128)(2,1)S(1)}, u32[]{:S(2)}, u32[]{:S(2)}) %collective-permute-start.5) | collective-permute-done | bytes 196640 | tf_op jit(solution)/shard_map/ppermute | solution.py:166
  43.4 2.9 %collective-permute-done.6.rest_7_ = bf16[256,384]{1,0:T(8,128)(2,1)S(1)} collective-permute-done((bf16[256,384]{1,0:T(8,128)(2,1)S(1)}, bf16[256,384]{1,0:T(8,128)(2,1)S(1)}, u32[]{:S(2)}, u32[]{:S(2)}) %collective-permute-start.6) | collective-permute-done | bytes 196640 | tf_op jit(solution)/shard_map/ppermute | solution.py:166
  46.3 1.7 %mix_grad.1 = (bf16[1024,384]{1,0:T(8,128)(2,1)S(1)}, bf16[512,384]{1,0:T(8,128)(2,1)S(1)}, bf16[512,384]{1,0:T(8,128)(2,1)S(1)}) custom-call(f32[1024,384]{1,0:T(8,128)S(1)} %gate.1.rest_0_, f32[1024,384]{1,0:T(8,128)S(1)} %get-tuple-element.47.rest_1_, bf16[384,384]{1,0:T(8,128)(2,1)S(1)} %get-tuple-element.40.dense_ref.rest_2_, ...), custom_call_target="tpu_custom_call" | custom-call | flops 805306368 | bytes 5799968 | tf_op jit(solution)/shard_map/mix_grad/pallas_call | solution.py:42
  48.1 1.8 %collective-permute-start.7 = (bf16[512,384]{1,0:T(8,128)(2,1)S(1)}, bf16[512,384]{1,0:T(8,128)(2,1)S(1)}, u32[]{:S(2)}, u32[]{:S(2)}) collective-permute-start(bf16[512,384]{1,0:T(8,128)(2,1)S(1)} %get-tuple-element.54), channel_id=1, source_target_pairs={{0,4},{4,0},{1,5},{5,1},{2,6},{6,2},{3,7},{7,3},{8,12},{12,8},{9,1... | collective-permute-start | bytes 1179656 | tf_op jit(solution)/shard_map/ppermute | solution.py:166
  50.2 1.5 %collective-permute-start.16 = (bf16[256,1024]{1,0:T(8,128)(2,1)S(1)}, bf16[256,1024]{1,0:T(8,128)(2,1)S(1)}, u32[]{:S(2)}, u32[]{:S(2)}) collective-permute-start(bf16[256,1024]{1,0:T(8,128)(2,1)S(1)} %get-tuple-element.64), channel_id=1, source_target_pairs={{0,2},{1,3},{2,0},{3,1},{4,6},{5,7},{6,4},{7,5},{8,10},{9,11},{10,... | collective-permute-start | bytes 1572872 | tf_op jit(solution)/shard_map/ppermute | solution.py:166
  51.7 2.8 %out_grad.1 = (f32[384,128]{1,0:T(8,128)S(1)}, f32[16,128]{1,0:T(8,128)S(1)}) custom-call(bf16[512,384]{1,0:T(8,128)(2,1)S(1)} %get-tuple-element.38.own_ref.rest_0_, bf16[512,384]{1,0:T(8,128)(2,1)S(1)} %collective-permute-done.got_ref.rest_1_, bf16[1024,384]{1,0:T(8,128)(2,1)S(1)} %get-tuple-element.55.rest_2_, ...), custom_call_target="tpu_custom_call" | custom-call | flops 805306368 | bytes 3350528 | tf_op jit(solution)/shard_map/out_grad/pallas_call | solution.py:42
  54.5 5.1 %collective-permute-done.7.got_ref = bf16[512,384]{1,0:T(8,128)(2,1)S(1)} collective-permute-done((bf16[512,384]{1,0:T(8,128)(2,1)S(1)}, bf16[512,384]{1,0:T(8,128)(2,1)S(1)}, u32[]{:S(2)}, u32[]{:S(2)}) %collective-permute-start.7) | collective-permute-done | bytes 393248 | tf_op jit(solution)/shard_map/ppermute | solution.py:166
  59.7 3.4 %in_grad.1 = (bf16[1024,384]{1,0:T(8,128)(2,1)}, bf16[400,128]{1,0:T(8,128)(2,1)S(1)}) custom-call(bf16[1024,384]{1,0:T(8,128)(2,1)S(1)} %bitcast.21, bf16[12,64,64]{2,1,0:T(8,128)(2,1)S(1)} %copy-done.8, bf16[512,384]{1,0:T(8,128)(2,1)S(1)} %get-tuple-element.53.own_ref, bf16[512,384]{1,0:T(8,128)(2,1)S(1)} %collective-permute-done.7.got_ref, ...), custom_call_target="tpu_custom_call" | custom-call | flops 1207959552 | bytes 2764800 | tf_op jit(solution)/shard_map/in_grad/pallas_call | solution.py:42
  65.1 1.8 %collective-permute-start.17 = (bf16[128,1024]{1,0:T(8,128)(2,1)S(1)}, bf16[128,1024]{1,0:T(8,128)(2,1)S(1)}, u32[]{:S(2)}, u32[]{:S(2)}) collective-permute-start(bf16[128,1024]{1,0:T(8,128)(2,1)S(1)} %get-tuple-element.66), channel_id=1, source_target_pairs={{0,4},{4,0},{1,5},{5,1},{2,6},{6,2},{3,7},{7,3},{8,12},{12,8},{9,1... | collective-permute-start | bytes 786440 | tf_op jit(solution)/shard_map/ppermute | solution.py:166
  68.1 2.4 %collective-permute-done.9 = bf16[400,128]{1,0:T(8,128)(2,1)S(1)} collective-permute-done((bf16[400,128]{1,0:T(8,128)(2,1)S(1)}, bf16[400,128]{1,0:T(8,128)(2,1)S(1)}, u32[]{:S(2)}, u32[]{:S(2)}) %collective-permute-start.9) | collective-permute-done | bytes 102432 | tf_op jit(solution)/shard_map/ppermute | solution.py:166
  70.6 3.9 %collective-permute-start.13 = (bf16[400,128]{1,0:T(8,128)(2,1)S(1)}, bf16[400,128]{1,0:T(8,128)(2,1)S(1)}, u32[]{:S(2)}, u32[]{:S(2)}) collective-permute-start(bf16[400,128]{1,0:T(8,128)(2,1)S(1)} %add_convert_fusion.1), channel_id=1, source_target_pairs={{0,24},{8,16},{16,8},{24,0},{1,25},{9,17},{17,9},{25,1},{2,26},{10... | collective-permute-start | bytes 307208 | tf_op jit(solution)/shard_map/ppermute | solution.py:166
  75.1 1.5 %collective-permute-start.18 = (bf16[32,1024]{1,0:T(8,128)(2,1)S(1)}, bf16[32,1024]{1,0:T(8,128)(2,1)S(1)}, u32[]{:S(2)}, u32[]{:S(2)}) collective-permute-start(bf16[32,1024]{1,0:T(8,128)(2,1)S(1)} %get-tuple-element.68), channel_id=1, source_target_pairs={{0,8},{8,0},{16,24},{24,16},{1,9},{9,1},{17,25},{25,17},{2,10},{10... | collective-permute-start | bytes 196616 | tf_op jit(solution)/shard_map/ppermute | solution.py:166
  76.6 2.9 %collective-permute-start.19 = (bf16[32,1024]{1,0:T(8,128)(2,1)S(1)}, bf16[32,1024]{1,0:T(8,128)(2,1)S(1)}, u32[]{:S(2)}, u32[]{:S(2)}) collective-permute-start(bf16[32,1024]{1,0:T(8,128)(2,1)S(1)} %get-tuple-element.69), channel_id=1, source_target_pairs={{0,16},{8,24},{16,0},{24,8},{1,17},{9,25},{17,1},{25,9},{2,18},{10... | collective-permute-start | bytes 196616 | tf_op jit(solution)/shard_map/ppermute | solution.py:166
  79.5 2.6 %collective-permute-start.20 = (bf16[32,1024]{1,0:T(8,128)(2,1)S(1)}, bf16[32,1024]{1,0:T(8,128)(2,1)S(1)}, u32[]{:S(2)}, u32[]{:S(2)}) collective-permute-start(bf16[32,1024]{1,0:T(8,128)(2,1)S(1)} %get-tuple-element.70), channel_id=1, source_target_pairs={{0,24},{8,16},{16,8},{24,0},{1,25},{9,17},{17,9},{25,1},{2,26},{10... | collective-permute-start | bytes 196616 | tf_op jit(solution)/shard_map/ppermute | solution.py:166
  82.1 4.9 %collective-permute-done.12 = bf16[400,128]{1,0:T(8,128)(2,1)S(1)} collective-permute-done((bf16[400,128]{1,0:T(8,128)(2,1)S(1)}, bf16[400,128]{1,0:T(8,128)(2,1)S(1)}, u32[]{:S(2)}, u32[]{:S(2)}) %collective-permute-start.12) | collective-permute-done | bytes 102432 | tf_op jit(solution)/shard_map/ppermute | solution.py:166
  87.0 1.6 %collective-permute-start.14 = (bf16[400,128]{1,0:T(8,128)(2,1)S(1)}, bf16[400,128]{1,0:T(8,128)(2,1)S(1)}, u32[]{:S(2)}, u32[]{:S(2)}) collective-permute-start(bf16[400,128]{1,0:T(8,128)(2,1)S(1)} %add_convert_fusion), channel_id=1, source_target_pairs={{0,4},{4,0},{1,5},{5,1},{2,6},{6,2},{3,7},{7,3},{8,12},{12,8},{9,1... | collective-permute-start | bytes 307208 | tf_op jit(solution)/shard_map/ppermute | solution.py:166
  88.7 2.2 %collective-permute-start.23 = (bf16[32,1024]{1,0:T(8,128)(2,1)S(1)}, bf16[32,1024]{1,0:T(8,128)(2,1)S(1)}, u32[]{:S(2)}, u32[]{:S(2)}) collective-permute-start(bf16[32,1024]{1,0:T(8,128)(2,1)S(1)} %z_sum.1.own_ref), channel_id=1, source_target_pairs={{0,24},{8,16},{16,8},{24,0},{1,25},{9,17},{17,9},{25,1},{2,26},{10... | collective-permute-start | bytes 196616 | tf_op jit(solution)/shard_map/ppermute | solution.py:166
  91.0 2.1 %collective-permute-start.21 = (bf16[32,1024]{1,0:T(8,128)(2,1)S(1)}, bf16[32,1024]{1,0:T(8,128)(2,1)S(1)}, u32[]{:S(2)}, u32[]{:S(2)}) collective-permute-start(bf16[32,1024]{1,0:T(8,128)(2,1)S(1)} %z_sum.1.own_ref), channel_id=1, source_target_pairs={{0,8},{8,0},{16,24},{24,16},{1,9},{9,1},{17,25},{25,17},{2,10},{10... | collective-permute-start | bytes 196616 | tf_op jit(solution)/shard_map/ppermute | solution.py:166
  93.1 1.9 %collective-permute-done.23.c_ref = bf16[32,1024]{1,0:T(8,128)(2,1)S(1)} collective-permute-done((bf16[32,1024]{1,0:T(8,128)(2,1)S(1)}, bf16[32,1024]{1,0:T(8,128)(2,1)S(1)}, u32[]{:S(2)}, u32[]{:S(2)}) %collective-permute-start.23) | collective-permute-done | bytes 65568 | tf_op jit(solution)/shard_map/ppermute | solution.py:166
  95.1 1.5 %collective-permute-done.22.b_ref = bf16[32,1024]{1,0:T(8,128)(2,1)S(1)} collective-permute-done((bf16[32,1024]{1,0:T(8,128)(2,1)S(1)}, bf16[32,1024]{1,0:T(8,128)(2,1)S(1)}, u32[]{:S(2)}, u32[]{:S(2)}) %collective-permute-start.22) | collective-permute-done | bytes 65568 | tf_op jit(solution)/shard_map/ppermute | solution.py:166
  96.6 1.6 %collective-permute-start.24 = (bf16[128,1024]{1,0:T(8,128)(2,1)S(1)}, bf16[128,1024]{1,0:T(8,128)(2,1)S(1)}, u32[]{:S(2)}, u32[]{:S(2)}) collective-permute-start(bf16[128,1024]{1,0:T(8,128)(2,1)S(1)} %z_join.1.own_ref), channel_id=1, source_target_pairs={{0,4},{4,0},{1,5},{5,1},{2,6},{6,2},{3,7},{7,3},{8,12},{12,8},{9,1... | collective-permute-start | bytes 786440 | tf_op jit(solution)/shard_map/ppermute | solution.py:166
  100.7 2.3 %collective-permute-done.24.got_ref = bf16[128,1024]{1,0:T(8,128)(2,1)S(1)} collective-permute-done((bf16[128,1024]{1,0:T(8,128)(2,1)S(1)}, bf16[128,1024]{1,0:T(8,128)(2,1)S(1)}, u32[]{:S(2)}, u32[]{:S(2)}) %collective-permute-start.24) | collective-permute-done | bytes 262176 | tf_op jit(solution)/shard_map/ppermute | solution.py:166
  (62 shorter events, 13.8 us)
Async XLA Ops:
  0.6 6.8 %copy-start = (bf16[64,12,12]{0,2,1:T(8,128)(2,1)S(1)}, bf16[64,12,12]{0,2,1:T(8,128)(2,1)}, u32[]{:S(2)}) copy-start(bf16[64,12,12]{0,2,1:T(8,128)(2,1)} %param.9) | copy-start | bytes 55300
  0.6 7.0 %copy-start.1 = (bf16[1024,1024]{1,0:T(8,128)(2,1)S(1)}, bf16[1024,1024]{1,0:T(8,128)(2,1)}, u32[]{:S(2)}) copy-start(bf16[1024,1024]{1,0:T(8,128)(2,1)} %rest_0_.1) | copy-start | bytes 6291460
  0.7 7.0 %copy-start.3 = (s32[1,1024]{1,0:T(1,128)S(1)}, s32[1,1024]{1,0:T(1,128)}, u32[]{:S(2)}) copy-start(s32[1,1024]{1,0:T(1,128)} %mask_ref.1) | copy-start | bytes 12292
  0.7 1.3 %copy-start.5 = (bf16[1,1024,384]{2,1,0:T(8,128)(2,1)S(1)}, bf16[1,1024,384]{2,1,0:T(8,128)(2,1)}, u32[]{:S(2)}) copy-start(bf16[1,1024,384]{2,1,0:T(8,128)(2,1)} %param.7) | copy-start | bytes 2359300
  4.4 12.2 %copy-start.4 = (bf16[4,4]{1,0:T(4,128)(2,1)S(1)}, bf16[4,4]{1,0:T(4,128)(2,1)}, u32[]{:S(2)}) copy-start(bf16[4,4]{1,0:T(4,128)(2,1)} %rest_3_.1) | copy-start | bytes 100
  4.4 12.1 %collective-permute-start = (bf16[512,384]{1,0:T(8,128)(2,1)S(1)}, bf16[512,384]{1,0:T(8,128)(2,1)S(1)}, u32[]{:S(2)}, u32[]{:S(2)}) collective-permute-start(bf16[512,384]{1,0:T(8,128)(2,1)S(1)} %get-tuple-element.39), channel_id=1, source_target_pairs={{0,4},{4,0},{1,5},{5,1},{2,6},{6,2},{3,7},{7,3},{8,12},{12,8},{9,1... | collective-permute-start | bytes 1179656 | tf_op jit(solution)/shard_map/ppermute | solution.py:166
  18.6 1.9 %collective-permute-start.1 = (bf16[256,384]{1,0:T(8,128)(2,1)S(1)}, bf16[256,384]{1,0:T(8,128)(2,1)S(1)}, u32[]{:S(2)}, u32[]{:S(2)}) collective-permute-start(bf16[256,384]{1,0:T(8,128)(2,1)S(1)} %get-tuple-element.44), channel_id=1, source_target_pairs={{0,1},{1,0},{2,3},{3,2},{4,5},{5,4},{6,7},{7,6},{8,9},{9,8},{10,11... | collective-permute-start | bytes 589832 | tf_op jit(solution)/shard_map/ppermute | solution.py:166
  18.6 7.8 %collective-permute-start.2 = (bf16[256,384]{1,0:T(8,128)(2,1)S(1)}, bf16[256,384]{1,0:T(8,128)(2,1)S(1)}, u32[]{:S(2)}, u32[]{:S(2)}) collective-permute-start(bf16[256,384]{1,0:T(8,128)(2,1)S(1)} %get-tuple-element.45), channel_id=1, source_target_pairs={{0,2},{1,3},{2,0},{3,1},{4,6},{5,7},{6,4},{7,5},{8,10},{9,11},{10,... | collective-permute-start | bytes 589832 | tf_op jit(solution)/shard_map/ppermute | solution.py:166
  20.4 9.3 %collective-permute-start.3 = (bf16[256,384]{1,0:T(8,128)(2,1)S(1)}, bf16[256,384]{1,0:T(8,128)(2,1)S(1)}, u32[]{:S(2)}, u32[]{:S(2)}) collective-permute-start(bf16[256,384]{1,0:T(8,128)(2,1)S(1)} %get-tuple-element.46), channel_id=1, source_target_pairs={{0,3},{1,2},{2,1},{3,0},{4,7},{5,6},{6,5},{7,4},{8,11},{9,10},{10,... | collective-permute-start | bytes 589832 | tf_op jit(solution)/shard_map/ppermute | solution.py:166
  33.7 16.2 %collective-permute-start.15 = (bf16[2,256,1024]{2,1,0:T(8,128)(2,1)S(1)}, bf16[2,256,1024]{2,1,0:T(8,128)(2,1)S(1)}, u32[]{:S(2)}, u32[]{:S(2)}) collective-permute-start(bf16[2,256,1024]{2,1,0:T(8,128)(2,1)S(1)} %get-tuple-element.62), channel_id=1, source_target_pairs={{0,1},{1,0},{2,3},{3,2},{4,5},{5,4},{6,7},{7,6},{8,9},{9,8},{10,11... | collective-permute-start | bytes 3145736 | tf_op jit(solution)/shard_map/ppermute | solution.py:166
  35.4 2.5 %collective-permute-start.4 = (bf16[256,384]{1,0:T(8,128)(2,1)S(1)}, bf16[256,384]{1,0:T(8,128)(2,1)S(1)}, u32[]{:S(2)}, u32[]{:S(2)}) collective-permute-start(bf16[256,384]{1,0:T(8,128)(2,1)S(1)} %get-tuple-element.50), channel_id=1, source_target_pairs={{0,1},{1,0},{2,3},{3,2},{4,5},{5,4},{6,7},{7,6},{8,9},{9,8},{10,11... | collective-permute-start | bytes 589832 | tf_op jit(solution)/shard_map/ppermute | solution.py:166
  35.7 7.7 %collective-permute-start.5 = (bf16[256,384]{1,0:T(8,128)(2,1)S(1)}, bf16[256,384]{1,0:T(8,128)(2,1)S(1)}, u32[]{:S(2)}, u32[]{:S(2)}) collective-permute-start(bf16[256,384]{1,0:T(8,128)(2,1)S(1)} %get-tuple-element.51), channel_id=1, source_target_pairs={{0,2},{1,3},{2,0},{3,1},{4,6},{5,7},{6,4},{7,5},{8,10},{9,11},{10,... | collective-permute-start | bytes 589832 | tf_op jit(solution)/shard_map/ppermute | solution.py:166
  37.4 8.9 %collective-permute-start.6 = (bf16[256,384]{1,0:T(8,128)(2,1)S(1)}, bf16[256,384]{1,0:T(8,128)(2,1)S(1)}, u32[]{:S(2)}, u32[]{:S(2)}) collective-permute-start(bf16[256,384]{1,0:T(8,128)(2,1)S(1)} %get-tuple-element.52), channel_id=1, source_target_pairs={{0,3},{1,2},{2,1},{3,0},{4,7},{5,6},{6,5},{7,4},{8,11},{9,10},{10,... | collective-permute-start | bytes 589832 | tf_op jit(solution)/shard_map/ppermute | solution.py:166
  48.1 11.6 %collective-permute-start.7 = (bf16[512,384]{1,0:T(8,128)(2,1)S(1)}, bf16[512,384]{1,0:T(8,128)(2,1)S(1)}, u32[]{:S(2)}, u32[]{:S(2)}) collective-permute-start(bf16[512,384]{1,0:T(8,128)(2,1)S(1)} %get-tuple-element.54), channel_id=1, source_target_pairs={{0,4},{4,0},{1,5},{5,1},{2,6},{6,2},{3,7},{7,3},{8,12},{12,8},{9,1... | collective-permute-start | bytes 1179656 | tf_op jit(solution)/shard_map/ppermute | solution.py:166
  50.1 9.5 %copy-start.6 = (bf16[1,1024,384]{2,1,0:T(8,128)(2,1)S(1)}, bf16[1,1024,384]{2,1,0:T(8,128)(2,1)}, u32[]{:S(2)}) copy-start(bf16[1,1024,384]{2,1,0:T(8,128)(2,1)} %param.7) | copy-start | bytes 2359300
  50.1 9.5 %copy-start.8 = (bf16[12,64,64]{2,1,0:T(8,128)(2,1)S(1)}, bf16[12,64,64]{2,1,0:T(8,128)(2,1)}, u32[]{:S(2)}) copy-start(bf16[12,64,64]{2,1,0:T(8,128)(2,1)} %in_ref.3) | copy-start | bytes 294916
  50.2 14.8 %collective-permute-start.16 = (bf16[256,1024]{1,0:T(8,128)(2,1)S(1)}, bf16[256,1024]{1,0:T(8,128)(2,1)S(1)}, u32[]{:S(2)}, u32[]{:S(2)}) collective-permute-start(bf16[256,1024]{1,0:T(8,128)(2,1)S(1)} %get-tuple-element.64), channel_id=1, source_target_pairs={{0,2},{1,3},{2,0},{3,1},{4,6},{5,7},{6,4},{7,5},{8,10},{9,11},{10,... | collective-permute-start | bytes 1572872 | tf_op jit(solution)/shard_map/ppermute | solution.py:166
  63.1 5.0 %collective-permute-start.10 = (bf16[400,128]{1,0:T(8,128)(2,1)S(1)}, bf16[400,128]{1,0:T(8,128)(2,1)S(1)}, u32[]{:S(2)}, u32[]{:S(2)}) collective-permute-start(bf16[400,128]{1,0:T(8,128)(2,1)S(1)} %get-tuple-element.60), channel_id=1, source_target_pairs={{0,3},{1,2},{2,1},{3,0},{4,7},{5,6},{6,5},{7,4},{8,11},{9,10},{10,... | collective-permute-start | bytes 307208 | tf_op jit(solution)/shard_map/ppermute | solution.py:166
  64.1 6.4 %collective-permute-start.9 = (bf16[400,128]{1,0:T(8,128)(2,1)S(1)}, bf16[400,128]{1,0:T(8,128)(2,1)S(1)}, u32[]{:S(2)}, u32[]{:S(2)}) collective-permute-start(bf16[400,128]{1,0:T(8,128)(2,1)S(1)} %get-tuple-element.60), channel_id=1, source_target_pairs={{0,2},{1,3},{2,0},{3,1},{4,6},{5,7},{6,4},{7,5},{8,10},{9,11},{10,... | collective-permute-start | bytes 307208 | tf_op jit(solution)/shard_map/ppermute | solution.py:166
  64.9 5.6 %collective-permute-start.8 = (bf16[400,128]{1,0:T(8,128)(2,1)S(1)}, bf16[400,128]{1,0:T(8,128)(2,1)S(1)}, u32[]{:S(2)}, u32[]{:S(2)}) collective-permute-start(bf16[400,128]{1,0:T(8,128)(2,1)S(1)} %get-tuple-element.60), channel_id=1, source_target_pairs={{0,1},{1,0},{2,3},{3,2},{4,5},{5,4},{6,7},{7,6},{8,9},{9,8},{10,11... | collective-permute-start | bytes 307208 | tf_op jit(solution)/shard_map/ppermute | solution.py:166
  65.1 10.0 %collective-permute-start.17 = (bf16[128,1024]{1,0:T(8,128)(2,1)S(1)}, bf16[128,1024]{1,0:T(8,128)(2,1)S(1)}, u32[]{:S(2)}, u32[]{:S(2)}) collective-permute-start(bf16[128,1024]{1,0:T(8,128)(2,1)S(1)} %get-tuple-element.66), channel_id=1, source_target_pairs={{0,4},{4,0},{1,5},{5,1},{2,6},{6,2},{3,7},{7,3},{8,12},{12,8},{9,1... | collective-permute-start | bytes 786440 | tf_op jit(solution)/shard_map/ppermute | solution.py:166
  70.6 9.0 %collective-permute-start.13 = (bf16[400,128]{1,0:T(8,128)(2,1)S(1)}, bf16[400,128]{1,0:T(8,128)(2,1)S(1)}, u32[]{:S(2)}, u32[]{:S(2)}) collective-permute-start(bf16[400,128]{1,0:T(8,128)(2,1)S(1)} %add_convert_fusion.1), channel_id=1, source_target_pairs={{0,24},{8,16},{16,8},{24,0},{1,25},{9,17},{17,9},{25,1},{2,26},{10... | collective-permute-start | bytes 307208 | tf_op jit(solution)/shard_map/ppermute | solution.py:166
  74.5 12.5 %collective-permute-start.12 = (bf16[400,128]{1,0:T(8,128)(2,1)S(1)}, bf16[400,128]{1,0:T(8,128)(2,1)S(1)}, u32[]{:S(2)}, u32[]{:S(2)}) collective-permute-start(bf16[400,128]{1,0:T(8,128)(2,1)S(1)} %add_convert_fusion.1), channel_id=1, source_target_pairs={{0,16},{8,24},{16,0},{24,8},{1,17},{9,25},{17,1},{25,9},{2,18},{10... | collective-permute-start | bytes 307208 | tf_op jit(solution)/shard_map/ppermute | solution.py:166
  74.5 12.5 %collective-permute-start.11 = (bf16[400,128]{1,0:T(8,128)(2,1)S(1)}, bf16[400,128]{1,0:T(8,128)(2,1)S(1)}, u32[]{:S(2)}, u32[]{:S(2)}) collective-permute-start(bf16[400,128]{1,0:T(8,128)(2,1)S(1)} %add_convert_fusion.1), channel_id=1, source_target_pairs={{0,8},{8,0},{16,24},{24,16},{1,9},{9,1},{17,25},{25,17},{2,10},{10... | collective-permute-start | bytes 307208 | tf_op jit(solution)/shard_map/ppermute | solution.py:166
  75.1 13.5 %collective-permute-start.18 = (bf16[32,1024]{1,0:T(8,128)(2,1)S(1)}, bf16[32,1024]{1,0:T(8,128)(2,1)S(1)}, u32[]{:S(2)}, u32[]{:S(2)}) collective-permute-start(bf16[32,1024]{1,0:T(8,128)(2,1)S(1)} %get-tuple-element.68), channel_id=1, source_target_pairs={{0,8},{8,0},{16,24},{24,16},{1,9},{9,1},{17,25},{25,17},{2,10},{10... | collective-permute-start | bytes 196616 | tf_op jit(solution)/shard_map/ppermute | solution.py:166
  76.6 12.0 %collective-permute-start.19 = (bf16[32,1024]{1,0:T(8,128)(2,1)S(1)}, bf16[32,1024]{1,0:T(8,128)(2,1)S(1)}, u32[]{:S(2)}, u32[]{:S(2)}) collective-permute-start(bf16[32,1024]{1,0:T(8,128)(2,1)S(1)} %get-tuple-element.69), channel_id=1, source_target_pairs={{0,16},{8,24},{16,0},{24,8},{1,17},{9,25},{17,1},{25,9},{2,18},{10... | collective-permute-start | bytes 196616 | tf_op jit(solution)/shard_map/ppermute | solution.py:166
  79.5 9.1 %collective-permute-start.20 = (bf16[32,1024]{1,0:T(8,128)(2,1)S(1)}, bf16[32,1024]{1,0:T(8,128)(2,1)S(1)}, u32[]{:S(2)}, u32[]{:S(2)}) collective-permute-start(bf16[32,1024]{1,0:T(8,128)(2,1)S(1)} %get-tuple-element.70), channel_id=1, source_target_pairs={{0,24},{8,16},{16,8},{24,0},{1,25},{9,17},{17,9},{25,1},{2,26},{10... | collective-permute-start | bytes 196616 | tf_op jit(solution)/shard_map/ppermute | solution.py:166
  87.0 11.1 %collective-permute-start.14 = (bf16[400,128]{1,0:T(8,128)(2,1)S(1)}, bf16[400,128]{1,0:T(8,128)(2,1)S(1)}, u32[]{:S(2)}, u32[]{:S(2)}) collective-permute-start(bf16[400,128]{1,0:T(8,128)(2,1)S(1)} %add_convert_fusion), channel_id=1, source_target_pairs={{0,4},{4,0},{1,5},{5,1},{2,6},{6,2},{3,7},{7,3},{8,12},{12,8},{9,1... | collective-permute-start | bytes 307208 | tf_op jit(solution)/shard_map/ppermute | solution.py:166
  88.7 6.4 %collective-permute-start.23 = (bf16[32,1024]{1,0:T(8,128)(2,1)S(1)}, bf16[32,1024]{1,0:T(8,128)(2,1)S(1)}, u32[]{:S(2)}, u32[]{:S(2)}) collective-permute-start(bf16[32,1024]{1,0:T(8,128)(2,1)S(1)} %z_sum.1.own_ref), channel_id=1, source_target_pairs={{0,24},{8,16},{16,8},{24,0},{1,25},{9,17},{17,9},{25,1},{2,26},{10... | collective-permute-start | bytes 196616 | tf_op jit(solution)/shard_map/ppermute | solution.py:166
  90.9 5.7 %collective-permute-start.22 = (bf16[32,1024]{1,0:T(8,128)(2,1)S(1)}, bf16[32,1024]{1,0:T(8,128)(2,1)S(1)}, u32[]{:S(2)}, u32[]{:S(2)}) collective-permute-start(bf16[32,1024]{1,0:T(8,128)(2,1)S(1)} %z_sum.1.own_ref), channel_id=1, source_target_pairs={{0,16},{8,24},{16,0},{24,8},{1,17},{9,25},{17,1},{25,9},{2,18},{10... | collective-permute-start | bytes 196616 | tf_op jit(solution)/shard_map/ppermute | solution.py:166
  91.0 5.5 %collective-permute-start.21 = (bf16[32,1024]{1,0:T(8,128)(2,1)S(1)}, bf16[32,1024]{1,0:T(8,128)(2,1)S(1)}, u32[]{:S(2)}, u32[]{:S(2)}) collective-permute-start(bf16[32,1024]{1,0:T(8,128)(2,1)S(1)} %z_sum.1.own_ref), channel_id=1, source_target_pairs={{0,8},{8,0},{16,24},{24,16},{1,9},{9,1},{17,25},{25,17},{2,10},{10... | collective-permute-start | bytes 196616 | tf_op jit(solution)/shard_map/ppermute | solution.py:166
  96.6 6.4 %collective-permute-start.24 = (bf16[128,1024]{1,0:T(8,128)(2,1)S(1)}, bf16[128,1024]{1,0:T(8,128)(2,1)S(1)}, u32[]{:S(2)}, u32[]{:S(2)}) collective-permute-start(bf16[128,1024]{1,0:T(8,128)(2,1)S(1)} %z_join.1.own_ref), channel_id=1, source_target_pairs={{0,4},{4,0},{1,5},{5,1},{2,6},{6,2},{3,7},{7,3},{8,12},{12,8},{9,1... | collective-permute-start | bytes 786440 | tf_op jit(solution)/shard_map/ppermute | solution.py:166
  (2 other events, 2.1 us)

commit v2 on v0

v2 whole, which is shorter than its diff:
```python
import functools

import jax
import jax.numpy as jnp
from jax import lax
from jax.experimental import pallas as pl
from jax.experimental.pallas import tpu as pltpu
from jax.sharding import PartitionSpec as P

F32 = jnp.float32
BF16 = jnp.bfloat16
VMEM_LIMIT = 24 * 1024 * 1024
PACK_LANES = 128
MIX_FLOPS = 600000000
OUT_FLOPS = 1
PACK_SUM_FLOPS = 1
X_FLOPS = 1
OWN_X_FLOPS = 4000000000


def dot(lhs, rhs, lhs_dim=1, rhs_dim=0):
    return lax.dot_general(
        lhs, rhs, (((lhs_dim,), (rhs_dim,)), ((), ())), preferred_element_type=F32
    )


def dot_exact(lhs, rhs, lhs_dim=1, rhs_dim=0):
    return lax.dot_general(
        lhs,
        rhs,
        (((lhs_dim,), (rhs_dim,)), ((), ())),
        precision=lax.Precision.HIGHEST,
        preferred_element_type=F32,
    )


def rows_of(shape):
    return lax.broadcasted_iota(jnp.int32, shape, 0)


def columns_of(shape):
    return lax.broadcasted_iota(jnp.int32, shape, 1)


def call(body, outs, args, scratch=(), flops=1, name=None):
    nbytes = sum(a.size * a.dtype.itemsize for a in list(args) + list(outs))
    return pl.pallas_call(
        body,
        out_shape=tuple(outs),
        in_specs=[pl.BlockSpec(memory_space=pltpu.VMEM)] * len(args),
        out_specs=tuple([pl.BlockSpec(memory_space=pltpu.VMEM)] * len(outs)),
        scratch_shapes=list(scratch),
        compiler_params=pltpu.CompilerParams(vmem_limit_bytes=VMEM_LIMIT),
        cost_estimate=pl.CostEstimate(flops=flops, bytes_accessed=1, transcendentals=0),
        name=name,
    )(*args)


def struct(shape, dtype=BF16):
    return jax.ShapeDtypeStruct(shape, dtype)


class Sizes:
    def __init__(self, tokens, chan_in, seq_count):
        self.positions, self.width = tokens.shape
        self.blocks, self.block = chan_in.shape[0], chan_in.shape[1]
        self.my_blocks = self.blocks // 2
        self.my_lanes = self.block // 2
        self.half = self.positions // 2
        self.quarter = self.positions // 4
        self.part = self.my_blocks * self.my_lanes
        self.seq = seq_count
        self.group = self.positions // seq_count
        self.direct = seq_count == 4
        self.fronts = 4 if self.direct else 2
        self.front = self.positions // self.fronts
        self.piece = self.group // self.fronts
        self.step = min(64, self.piece)
        self.chunk = self.step * seq_count
        self.pack_in = self.width // 2
        self.pack_out = 16 * (self.width // PACK_LANES)
        self.pack_rows = self.pack_in + self.pack_out + max(16, seq_count)
        self.share = self.pack_rows // seq_count


def lane_masks(z):
    shape = (z.width, 2 * z.part)
    row, column = rows_of(shape), columns_of(shape)
    left = column < z.part
    place = jnp.where(left, column, column - z.part)
    same = (row // z.block) == (place // z.my_lanes)
    return same & left, same & jnp.logical_not(left)


def in_matrices(z, in_ref, lane_base):
    chan = lax.axis_index("chan")
    blocks = in_ref[pl.ds(chan * z.my_blocks, z.my_blocks)].reshape(z.width, z.block)
    column = columns_of((z.block, 2 * z.part))
    pick = rows_of((z.block, 2 * z.part)) == lane_base + (column & (z.my_lanes - 1))
    spread = dot(blocks, pick.astype(BF16))
    left, right = lane_masks(z)
    return jnp.where(left, spread, 0.0).astype(BF16), jnp.where(right, spread, 0.0).astype(BF16)


def lane_of_channel(z, shape, axis):
    index = lax.broadcasted_iota(jnp.int32, shape, axis)
    lane = (index * 5462) >> 16
    return lane, index - z.blocks * lane


def out_mask(z):
    shape = (z.blocks * z.my_lanes, z.width)
    lane, _ = lane_of_channel(z, shape, 1)
    return (rows_of(shape) & (z.my_lanes - 1)) == lane


def out_matrix(z, factors):
    shape = (z.blocks, z.width)
    _, entry = lane_of_channel(z, shape, 1)
    spread = dot(factors, (rows_of(shape) == entry).astype(BF16))
    return jnp.where(out_mask(z), spread, 0.0).astype(BF16)


def position_masks(z):
    shape = (z.chunk, z.chunk)
    row, column = rows_of(shape), columns_of(shape)
    same = (row & (z.step - 1)) == (column // z.seq)
    blocks = (z.chunk, z.seq)
    of_a = (rows_of(blocks) // z.step) == columns_of(blocks)
    turned = (z.seq, z.chunk)
    of_a2 = (columns_of(turned) & (z.seq - 1)) == rows_of(turned)
    return same, of_a, of_a2


def position_matrix(z, factor):
    same, of_a, of_a2 = position_masks(z)
    by_row = dot(of_a.astype(BF16), factor).astype(BF16)
    return jnp.where(same, dot(by_row, of_a2.astype(BF16)), 0.0).astype(BF16)


def split_blocks(z, full_ref, refs):
    if not z.direct:
        refs[0][...] = full_ref[...]
        return
    mine = lax.axis_index("seq")
    stay_ref, mate_ref, far_ref = refs
    stay_ref[...] = full_ref[mine]
    mate_ref[...] = full_ref[mine ^ 1]
    far_ref[0] = full_ref[mine ^ 2]
    far_ref[1] = full_ref[mine ^ 3]


def block_outs(z, rows):
    if not z.direct:
        return [struct((z.seq, rows, z.width))]
    return [struct((rows, z.width))] * 2 + [struct((2, rows, z.width))]


def own_mate_kernel(*refs):
    rows, out_ref = refs[0].shape[0], refs[-1]
    for c, ref in enumerate(refs[:-1]):
        out_ref[c * rows : (c + 1) * rows, :] = ref[...]


def mate_kernel(count, *refs):
    rows, out_ref = refs[0].shape[1], refs[-1]
    for c in range(count):
        out_ref[c * rows : (c + 1) * rows, :] = refs[c][1]


def exchange_blocks(z, chunks, fars, after):
    if not z.direct:
        return [lax.all_to_all(c[0], "seq", split_axis=0, concat_axis=0, tiled=True) for c in chunks]
    whole = [struct((z.group, z.width))]
    mates = [mate for _, mate, _ in chunks]
    if len(mates) > 1:
        mates = call(own_mate_kernel, whole, mates, name="own_mate")
    for_mate = call(functools.partial(mate_kernel, len(chunks)), whole, fars + [after], name="mate")
    return [stay for stay, _, _ in chunks] + fars + [swap(mates[0], "seq", 1), swap(for_mate[0], "seq", 1)]


def send_far(z, blocks):
    return swap(blocks[2], "seq", 2) if z.direct else blocks[0]


def join_blocks(z, refs, full_ref):
    count = len(refs) // 2 - 1 if z.direct else len(refs)
    size = z.group // count
    mine = lax.axis_index("seq")
    for c in range(count):
        rows = slice(c * size, (c + 1) * size)
        if not z.direct:
            full_ref[:, rows, :] = refs[c][...]
            continue
        full_ref[mine, rows, :] = refs[c][...]
        full_ref[mine ^ 1, rows, :] = refs[2 * count][rows, :]
        full_ref[mine ^ 2, rows, :] = refs[count + c][0]
        full_ref[mine ^ 3, rows, :] = refs[2 * count + 1][rows, :]


def swap(value, axis, step):
    size = lax.axis_size(axis)
    return lax.ppermute(value, axis, [(i, i ^ step) for i in range(size)])


def swap_both(value, chan_step, seq_step):
    seq = lax.axis_size("seq")
    pairs = [
        (c * seq + s, (c ^ chan_step) * seq + (s ^ seq_step))
        for c in range(lax.axis_size("chan"))
        for s in range(seq)
    ]
    return lax.ppermute(value, ("chan", "seq"), pairs)


def quarters(z, ref, c):
    low = ref[c * z.half : c * z.half + z.quarter, :]
    return low, ref[c * z.half + z.quarter : (c + 1) * z.half, :]


def front_rows(z, ref, c):
    middle = c * z.front + z.front // 2
    return ref[c * z.front : middle, :], ref[middle : (c + 1) * z.front, :]


def first_kernel(z, c, x_ref, in_ref, out_ref):
    chan = lax.axis_index("chan")
    lower, upper = in_matrices(z, in_ref, (1 - chan) * z.my_lanes)
    low, high = front_rows(z, x_ref, c)
    out_ref[...] = (dot(low, lower) + dot(high, upper)).astype(BF16)


def prepare_kernel(z, x_ref, in_ref, head_ref, mask_ref, seq_ref, out_ref, after_ref, *outs):
    own_refs, (up_ref, turn_ref, pad_ref, win_ref) = outs[: z.fronts], outs[z.fronts :]
    chan = lax.axis_index("chan")
    lower, upper = in_matrices(z, in_ref, chan * z.my_lanes)
    win_ref[0], win_ref[1] = lower, upper
    win_ref[2], win_ref[3] = in_matrices(z, in_ref, (1 - chan) * z.my_lanes)
    for c, ref in enumerate(own_refs):
        low, high = front_rows(z, x_ref, c)
        ref[...] = (dot(low, lower) + dot(high, upper)).astype(BF16)
    lines = jnp.broadcast_to(mask_ref[...].astype(F32), (16, z.positions)).astype(BF16)
    ones = jnp.full((16, z.width), 1.0 / 16.0, BF16)
    mask = dot(lines, ones, 0, 0)
    up_ref[...] = (mask * head_ref[...].astype(F32)).astype(BF16)
    turn_ref[...] = jnp.transpose(seq_ref[...])
    pad_ref[...] = jnp.zeros_like(pad_ref)
    dense = out_matrix(z, out_ref[...])
    for base in range(2):
        pad_ref[base ^ chan, z.part : 2 * z.part, :] = dense[base * z.part : (base + 1) * z.part, :]


def channel_mix_kernel(z, c, own_ref, got_ref, pad_ref, up_ref, so_ref, *rest):
    mix_ref, gated_ref = rest[:2]
    refs, rows_ref = rest[2:-1], rest[-1]
    own, got = own_ref[...], got_ref[...]
    rows = z.front // 2
    low = dot(own, pad_ref[0, z.part :, :]) + dot(got, pad_ref[1, z.part :, :])
    high = dot(own, pad_ref[0, : 2 * z.part, :]) + dot(got, pad_ref[1, : 2 * z.part, :])
    for at, values in ((0, low), (rows, high)):
        rounded = values.astype(BF16)
        mix_ref[at : at + rows, :] = rounded
        mixed = rounded.astype(F32)
        upstream = up_ref[c * z.front + at : c * z.front + at + rows, :].astype(F32)
        gated = upstream * (mixed * jax.nn.sigmoid(mixed))
        gated_ref[at : at + rows, :] = gated.astype(BF16)
    matrix = position_matrix(z, so_ref[...])
    for j in range(z.front // z.chunk):
        out = dot(matrix, gated_ref[j * z.chunk : (j + 1) * z.chunk, :]).astype(BF16)
        rows_ref[:, j * z.step : (j + 1) * z.step, :] = out.reshape(z.seq, z.step, z.width)
    split_blocks(z, rows_ref, refs)


def row_mix_kernel(z, turn_ref, *rest):
    mixes, (all0_ref, all1_ref), refs, rows_ref = rest[: z.fronts], rest[z.fronts :][:2], rest[z.fronts + 2 : -1], rest[-1]
    per_half = z.fronts // 2
    for c, mix_ref in enumerate(mixes):
        at = (c % per_half) * z.front
        (all0_ref, all1_ref)[c // per_half][at : at + z.front, :] = mix_ref[...]
    out = dot(turn_ref[:, : z.half], all0_ref[...]) + dot(turn_ref[:, z.half :], all1_ref[...])
    rows_ref[...] = out.astype(BF16).reshape(z.seq, z.group, z.width)
    split_blocks(z, rows_ref, refs)


def seq_grad_kernel(z, count, mix0_ref, mix1_ref, *rest):
    refs, all_ref, outs, rows_ref = rest[:count], rest[count], rest[count + 1 : -1], rest[-1]
    join_blocks(z, refs, rows_ref)
    all_ref[...] = rows_ref[...].reshape(z.positions, z.width)
    if not z.direct:
        for c, mix_ref in enumerate((mix0_ref, mix1_ref)):
            outs[0][c * z.half : (c + 1) * z.half, :] = dot(mix_ref[...], all_ref[...], 1, 1)
        return
    core_products(z, 1 - (lax.axis_index("seq") & 1), (mix0_ref, mix1_ref), all_ref, outs)


def core_products(z, core, mixes, all_ref, outs):
    lines = z.group // 2
    for k, out in enumerate(outs):
        at = pl.multiple_of(core * z.group + (k & 1) * lines, lines)
        out[...] = dot(mixes[k >> 1][pl.ds(at, lines), :], all_ref[...], 1, 1).astype(BF16)


def own_product_kernel(z, mix0_ref, mix1_ref, all_ref, *outs):
    core_products(z, lax.axis_index("seq") & 1, (mix0_ref, mix1_ref), all_ref, outs)


def seq_part_kernel(z, seq_ref, rows_ref, mix0_ref, mix1_ref, up_ref, after_ref, part_ref, gate_ref):
    part_ref[...] = dot(seq_ref[...], rows_ref[...])
    for c, mix_ref in enumerate((mix0_ref, mix1_ref)):
        at = slice(c * z.half, (c + 1) * z.half)
        mixed = mix_ref[...].astype(F32)
        sig = jax.nn.sigmoid(mixed)
        gate_ref[at, :] = up_ref[at, :].astype(F32) * (sig * (1.0 + mixed * (1.0 - sig)))


def turn_kernel(z, x_ref, *rest):
    owns, gots = rest[: z.fronts], rest[z.fronts : 2 * z.fronts]
    xt_ref, ot_ref, gt_ref = rest[2 * z.fronts + 1 :]
    xt_ref[...] = jnp.transpose(x_ref[...])
    rows = z.front // 2
    for refs, out_ref in ((owns, ot_ref), (gots, gt_ref)):
        for c, ref in enumerate(refs):
            out_ref[:, c * rows : (c + 1) * rows] = jnp.transpose(ref[...])


def mix_grad_kernel(z, gate_ref, part_ref, pad_ref, so_ref, *rest):
    refs, (mixg_ref, own_ref, other_ref, spread_ref, joined_ref) = rest[:-5], rest[-5:]
    matrix = position_matrix(z, so_ref[...])
    join_blocks(z, refs, joined_ref)
    for j in range(z.positions // z.chunk):
        rows = joined_ref[:, j * z.step : (j + 1) * z.step, :].reshape(z.chunk, z.width)
        at = slice(j * z.chunk, (j + 1) * z.chunk)
        spread_ref[at, :] = rows
        gate = gate_ref[at, :] * dot(matrix, rows, 0, 0)
        mixg_ref[at, :] = (gate + part_ref[at, :]).astype(BF16)
    for c in range(2):
        low, high = quarters(z, mixg_ref, c)
        for base, ref in ((1, other_ref), (0, own_ref)):
            first = dot(low, pad_ref[base, z.part :, :], 1, 1)
            total = first + dot(high, pad_ref[base, : 2 * z.part, :], 1, 1)
            ref[c * z.quarter : (c + 1) * z.quarter, :] = total.astype(BF16)


def in_products(z, xt_ref, grad_ref, lane_base):
    low = high = None
    for c in range(2):
        at = c * z.half
        grad = grad_ref[c * z.quarter : (c + 1) * z.quarter, :]
        first = dot(xt_ref[:, at : at + z.quarter], grad)
        second = dot(xt_ref[:, at + z.quarter : at + z.half], grad)
        low = first if low is None else low + first
        high = second if high is None else high + second
    left, right = lane_masks(z)
    products = jnp.where(left, low, jnp.where(right, high, 0.0)).astype(BF16)
    shape = (2 * z.part, PACK_LANES)
    lane = lane_base + (rows_of(shape) & (z.my_lanes - 1))
    column = columns_of(shape)
    packed = dot(products[: z.pack_in, :], (column == lane).astype(BF16))
    return packed + dot(products[z.pack_in :, :], (column == lane + z.block).astype(BF16))


def out_grad_kernel(z, *rest):
    ot_ref, gt_ref, xt_ref, mixg_ref, owng_ref = rest[:5]
    gateds, spread_ref = rest[5 : 5 + z.fronts], rest[5 + z.fronts]
    in_ref, small_ref = rest[6 + z.fronts :]
    chan = lax.axis_index("chan")
    in_ref[...] = in_products(z, xt_ref, owng_ref, chan * z.my_lanes)
    shape = (16, z.width)
    _, entry = lane_of_channel(z, shape, 1)
    to_entry = (rows_of(shape) == entry).astype(BF16)
    shape = (z.part, z.width)
    lane, _ = lane_of_channel(z, shape, 1)
    mask = (rows_of(shape) & (z.my_lanes - 1)) == lane
    sides = []
    for turned_ref in (ot_ref, gt_ref):
        kept = None
        for c in range(z.fronts):
            low, high = front_rows(z, mixg_ref, c)
            at = slice(c * z.front // 2, (c + 1) * z.front // 2)
            both = dot(turned_ref[: z.part, at], low) + dot(turned_ref[z.part :, at], high)
            kept = both if kept is None else kept + both
        sides.append(dot(to_entry, jnp.where(mask, kept, 0.0).astype(BF16), 1, 1))
    both = jnp.concatenate(
        [jnp.where(chan == 0, sides[0], sides[1]), jnp.where(chan == 0, sides[1], sides[0])], axis=1
    ).astype(BF16)
    for j in range(z.width // PACK_LANES):
        small_ref[j * 16 : (j + 1) * 16, :] = both[:, j * PACK_LANES : (j + 1) * PACK_LANES]
    same, of_a, of_a2 = position_masks(z)
    total = jnp.zeros((z.chunk, z.chunk), F32)
    for c, gated_ref in enumerate(gateds):
        for j in range(z.front // z.chunk):
            at = c * z.front + j * z.chunk
            gated = gated_ref[j * z.chunk : (j + 1) * z.chunk, :]
            total = total + dot(spread_ref[at : at + z.chunk, :], gated, 1, 1)
    total = jnp.where(same, total, 0.0)
    shape = (z.chunk, PACK_LANES)
    to_a2 = ((rows_of(shape) & (z.seq - 1)) == columns_of(shape)).astype(F32)
    tall = (max(16, z.seq), z.chunk)
    to_a = ((columns_of(tall) // z.step) == rows_of(tall)).astype(F32)
    small_ref[z.pack_out :, :] = dot_exact(to_a, dot_exact(total, to_a2)).astype(BF16)


def pack_kernel(z, xt_ref, got_ref, in_ref, small_ref, after0_ref, after1_ref, *rest):
    outs, pack_ref = rest[:-1], rest[-1]
    there = (1 - lax.axis_index("chan")) * z.my_lanes
    pack_ref[: z.pack_in, :] = (in_ref[...] + in_products(z, xt_ref, got_ref, there)).astype(BF16)
    pack_ref[z.pack_in :, :] = small_ref[...]
    if not z.direct:
        outs[0][...] = pack_ref[...]
        return
    mine = lax.axis_index("seq")
    for step, ref in enumerate(outs):
        ref[...] = pack_ref[pl.ds(pl.multiple_of((mine ^ step) * z.share, z.share), z.share), :]


def own_x_grad_kernel(z, win_ref, own_ref, after_ref, part_ref, token_ref):
    for c in range(2):
        rows = slice(c * z.quarter, (c + 1) * z.quarter)
        for side in range(2):
            at = c * z.half + side * z.quarter
            part_ref[at : at + z.quarter, :] = dot(own_ref[rows, :], win_ref[side], 1, 1)
    token_ref[...] = part_ref[: token_ref.shape[0], : token_ref.shape[1]]


def x_grad_kernel(z, win_ref, part_ref, got_ref, after_ref, xg_ref, token_ref):
    for c in range(2):
        rows = slice(c * z.quarter, (c + 1) * z.quarter)
        for side in range(2):
            at = slice(c * z.half + side * z.quarter, c * z.half + (side + 1) * z.quarter)
            total = part_ref[at, :] + dot(got_ref[rows, :], win_ref[2 + side], 1, 1)
            xg_ref[at, :] = total.astype(BF16)
    token_ref[...] = xg_ref[: token_ref.shape[0], : token_ref.shape[1]]


def unpack(z, sides, in_ref, out_ref, second_ref):
    per_side = z.my_blocks // 2
    for half, side in enumerate(sides):
        lanes = slice(half * z.my_lanes, (half + 1) * z.my_lanes)
        for b in range(z.my_blocks):
            at, base = (b % per_side) * z.block, (b // per_side) * z.block
            in_ref[half * z.my_blocks + b] = side[at : at + z.block, base : base + z.block]
        for b in range(z.blocks):
            at = z.pack_in + 16 * (b * z.my_lanes // PACK_LANES)
            base = b * z.my_lanes % PACK_LANES
            out_ref[b, :, lanes] = side[at : at + z.blocks, base : base + z.my_lanes]
    at = z.pack_in + z.pack_out
    second_ref[...] = sides[0][at : at + z.seq, : z.seq] + sides[1][at : at + z.seq, : z.seq]


def sum_pairs(parts):
    parts = [part.astype(F32) for part in parts]
    while len(parts) > 1:
        parts = [parts[i] + parts[i + 1] for i in range(0, len(parts), 2)]
    return parts[0]


def pair_sum_kernel(a_ref, b_ref, c_ref, d_ref, out_ref):
    out_ref[...] = sum_pairs([a_ref[...], b_ref[...], c_ref[...], d_ref[...]]).astype(out_ref.dtype)


def core_sum_kernel(*refs):
    keeps, gots, (keep0_ref, keep1_ref, send0_ref, send1_ref, all_ref) = refs[:4], refs[4:8], refs[8:]
    x, chan = lax.axis_index("seq") >> 1, lax.axis_index("chan")
    rows, half = all_ref.shape[1], all_ref.shape[2] // 2
    for k in range(4):
        all_ref[k] = keeps[k][...].astype(F32) + gots[k][...].astype(F32)
    for step in range(2):
        at = slice(step * rows, (step + 1) * rows)
        keep0_ref[at, :] = all_ref[2 * (x ^ step) + chan, :, :half]
        send0_ref[at, :] = all_ref[2 * (x ^ step) + (1 - chan), :, :half].astype(BF16)
        keep1_ref[at, :] = all_ref[2 * x + (chan ^ step), :, half:]
        send1_ref[at, :] = all_ref[2 * (1 - x) + (chan ^ step), :, half:].astype(BF16)


def side_sum_kernel(keep0_ref, got0_ref, keep1_ref, got1_ref, after_ref, mine_ref, send0_ref, send1_ref):
    rows, half = send0_ref.shape
    mine_ref[:, :half] = keep0_ref[:rows, :] + got0_ref[:rows, :].astype(F32)
    mine_ref[:, half:] = keep1_ref[:rows, :] + got1_ref[:rows, :].astype(F32)
    send0_ref[...] = (keep0_ref[rows:, :] + got0_ref[rows:, :].astype(F32)).astype(BF16)
    send1_ref[...] = (keep1_ref[rows:, :] + got1_ref[rows:, :].astype(F32)).astype(BF16)


def plane_sum_kernel(rows, keep_ref, got0_ref, got1_ref, after_ref, *outs):
    dp = lax.axis_index("dp")
    blocks = keep_ref.shape[1] // PACK_LANES
    for step, out in enumerate(outs):
        at = pl.ds(pl.multiple_of((dp ^ step) * rows, rows), rows)
        for j in range(blocks):
            got_ref, there = (got0_ref, j) if j < blocks // 2 else (got1_ref, j - blocks // 2)
            got = got_ref[at, there * PACK_LANES : (there + 1) * PACK_LANES].astype(F32)
            total = keep_ref[at, j * PACK_LANES : (j + 1) * PACK_LANES] + got
            out[j * rows : (j + 1) * rows, :] = total.astype(BF16)


def pack_sum_kernel(a_ref, b_ref, c_ref, d_ref, out_ref):
    out_ref[...] = sum_pairs([a_ref[...], b_ref[...], c_ref[...], d_ref[...]]).astype(BF16)


def z_sum_kernel(own_ref, a_ref, b_ref, c_ref, small_ref, out_ref):
    rows = own_ref.shape[0]
    out_ref[:rows, :] = sum_pairs([own_ref[...], a_ref[...], b_ref[...], c_ref[...]]).astype(BF16)
    out_ref[rows:, :] = small_ref[...]


def pass_on_kernel(line_ref, after_ref, out_ref):
    out_ref[...] = line_ref[...]


def line_sum_kernel(z, *refs):
    out_ref = refs[8]
    rows = refs[0].shape[0] - z.share
    for there in range(2):
        at = pl.multiple_of((lax.axis_index("chan") ^ there) * z.share, z.share)
        total = sum_pairs([ref[rows:, :] for ref in refs[4 * there : 4 * there + 4]])
        out_ref[pl.ds(at, z.share), :] = total.astype(BF16)


def last_kernel(z, rows, *refs):
    lines, smalls = (refs[:4], refs[4:8]), refs[8:12]
    first_ref, in_ref, out_ref, second_ref, all_ref = refs[12:]
    chan, dp, mine = lax.axis_index("chan"), lax.axis_index("dp"), lax.axis_index("seq")
    for there in range(2):
        for step in range(4):
            to = pl.ds(pl.multiple_of(((chan ^ there) * 4 + (dp ^ step)) * rows, rows), rows)
            for j in range(first_ref.shape[1] // PACK_LANES):
                lanes = slice(j * PACK_LANES, (j + 1) * PACK_LANES)
                values = lines[there][step][j * rows : (j + 1) * rows, :]
                first_ref[to, lanes] = values.astype(F32)
    for step in range(4):
        at = pl.ds(pl.multiple_of((mine ^ step) * z.share, z.share), z.share)
        for half in range(2):
            values = smalls[step][half * z.share : (half + 1) * z.share, :]
            all_ref[half, at, :] = values.astype(F32)
    unpack(z, [all_ref[0], all_ref[1]], in_ref, out_ref, second_ref)


def pack_last_kernel(z, own_ref, got_ref, in_ref, out_ref, second_ref):
    chan = lax.axis_index("chan")
    own, got = own_ref[...], got_ref[...]
    unpack(z, [jnp.where(chan == 0, own, got), jnp.where(chan == 0, got, own)], in_ref, out_ref, second_ref)


def sum_cores(keeps, sends):
    rows, width = sends[0].shape
    half = (2 * rows, width // 2)
    return call(
        core_sum_kernel,
        [struct(half, F32)] * 2 + [struct(half)] * 2,
        list(keeps) + [swap(block, "seq", 1) for block in sends],
        [pltpu.VMEM((4, rows, width), F32)],
        name="core_sum",
    )


def sum_factors(z, core_sums, pack_after, mix_after, small_after, outs):
    keep0, keep1, send0, send1 = core_sums
    rows, width = keep0.shape[0] // 2, 2 * keep0.shape[1]
    bind = functools.partial
    mine, send0, send1 = call(
        side_sum_kernel,
        [struct((rows, width), F32)] + [struct((rows, width // 2))] * 2,
        [keep0, swap(send0, "chan", 1), keep1, swap(send1, "seq", 2), mix_after],
        name="side_sum",
    )
    lines = rows // 4
    tall = lines * (width // PACK_LANES)
    parts = call(
        bind(plane_sum_kernel, lines),
        [struct((tall, PACK_LANES))] * 4,
        [mine, swap(send0, "seq", 2), swap(send1, "chan", 1), small_after],
        name="plane_sum",
    )
    packs, x_grad, x_done = pack_after(parts[0])
    packs = [packs[0]] + [swap(packs[step], "seq", step) for step in range(1, 4)]
    (pack,) = call(
        pack_sum_kernel, [struct((z.share, PACK_LANES))], packs, flops=PACK_SUM_FLOPS, name="pack_sum"
    )
    parts = [parts[0]] + [swap(parts[step], "dp", step) for step in range(1, 4)]
    (own,) = call(
        z_sum_kernel,
        [struct((tall + z.share, PACK_LANES))],
        list(parts) + [pack],
        name="z_sum",
    )
    own_lines = [own] + [swap(own, "dp", step) for step in range(1, 4)]
    passed = list(own_lines)
    (passed[3],) = call(pass_on_kernel, [struct(own.shape)], [own_lines[3], x_done], name="pass_on")
    got_lines = [swap(line, "chan", 1) for line in passed]
    (small,) = call(
        bind(line_sum_kernel, z), [struct((2 * z.share, PACK_LANES))], own_lines + got_lines, name="line_sum"
    )
    smalls = [small] + [swap(small, "seq", step) for step in range(1, 4)]
    return x_grad, *call(
        bind(last_kernel, z, lines),
        [struct((8 * lines, width), F32)] + outs,
        own_lines + got_lines + smalls,
        [pltpu.VMEM((2, z.pack_rows, PACK_LANES), F32)],
        name="last",
    )


def sum_factors_plain(z, first, pack, outs):
    first = lax.psum_scatter(first, "seq", scatter_dimension=0, tiled=True)
    first = lax.psum(first, ("dp", "chan"))
    pack = lax.psum(pack.astype(F32), ("dp", "seq"))
    got = swap(pack, "chan", 1)
    return [first] + list(call(functools.partial(pack_last_kernel, z), outs, [pack, got], name="last"))


def per_device(tokens, chan_in, chan_out, seq_in, seq_out, head_grad, masked):
    seq_count = lax.axis_size("seq")
    chan_index = lax.axis_index("chan")
    tokens, head_grad = tokens[0], head_grad[0]
    z = Sizes(tokens, chan_in, seq_count)
    wide, chunk = (z.positions, z.width), (z.half, z.width)
    front = (z.front // 2, 2 * z.part)
    bind = functools.partial

    others = [
        call(bind(first_kernel, z, c), [struct(front)], [tokens, chan_in], name="first_mix")[0]
        for c in range(z.fronts)
    ]
    gots = [swap(other, "chan", 1) for other in others]

    factors = lax.dynamic_slice_in_dim(chan_out, chan_index * z.my_lanes, z.my_lanes, 0)
    factors = jnp.transpose(factors, (1, 0, 2)).reshape(z.blocks * z.my_lanes, z.blocks)
    *owns, upstream, turned, pads, in_mats = call(
        bind(prepare_kernel, z),
        [struct(front)] * z.fronts
        + [
            struct(wide),
            struct(seq_in.shape),
            struct((2, 3 * z.part, z.width)),
            struct((4, z.width, 2 * z.part)),
        ],
        [tokens, chan_in, head_grad, masked, seq_in, factors, others[-1]],
        name="prepare",
    )
    mixes, gateds, row_grads, fars = [], [], [], []
    for c in range(z.fronts):
        mix, gated, *row_grad = call(
            bind(channel_mix_kernel, z, c),
            [struct((z.front, z.width))] * 2 + block_outs(z, z.piece),
            [owns[c], gots[c], pads, upstream, seq_out],
            [pltpu.VMEM((z.seq, z.piece, z.width), BF16)],
            name="channel_mix",
        )
        mixes.append(mix)
        gateds.append(gated)
        row_grads.append(row_grad)
        fars.append(send_far(z, row_grad))
    joined_scratch = pltpu.VMEM((z.seq, z.group, z.width), BF16)
    mix0, mix1, *row_mix = call(
        bind(row_mix_kernel, z),
        [struct(chunk)] * 2 + block_outs(z, z.group),
        [turned] + mixes,
        [joined_scratch],
        name="row_mix",
    )
    mixes = [mix0, mix1]
    row_grads = exchange_blocks(z, row_grads, fars, row_mix[0])
    if z.direct:
        outs = [struct((z.group // 2, seq_in.shape[1]))] * 4
    else:
        outs = [struct(seq_in.shape, F32)]
    all_rows, *first_parts = call(
        bind(seq_grad_kernel, z, len(row_grads)),
        [struct(wide)] + outs,
        mixes + row_grads,
        [joined_scratch],
        name="seq_grad",
    )
    after = upstream
    if z.direct:
        keeps = call(bind(own_product_kernel, z), outs, mixes + [all_rows], name="own_product")
        core_sums = sum_cores(keeps, first_parts)
        after = core_sums[0]
    seq_part, gate = call(
        bind(seq_part_kernel, z),
        [struct(wide, F32)] * 2,
        [seq_in, all_rows] + mixes + [upstream, after],
        name="seq_part",
    )
    tokens_t, own_t, got_t = call(
        bind(turn_kernel, z),
        [struct((z.width, z.positions))] + [struct((2 * z.part, z.half))] * 2,
        [tokens] + owns + gots + [seq_part],
        name="turn",
    )
    spread = exchange_blocks(z, [row_mix], [send_far(z, row_mix)], tokens_t)
    mix_grad, own_grad, other_grad, spread = call(
        bind(mix_grad_kernel, z),
        [struct(wide), struct((z.half, 2 * z.part)), struct((z.half, 2 * z.part)), struct(wide)],
        [gate, seq_part, pads, seq_out] + spread,
        [joined_scratch],
        flops=MIX_FLOPS,
        name="mix_grad",
    )
    got_grad = swap(other_grad, "chan", 1)
    in_part, small = call(
        bind(out_grad_kernel, z),
        [struct((z.pack_in, PACK_LANES), F32), struct((z.pack_rows - z.pack_in, PACK_LANES))],
        [own_t, got_t, tokens_t, mix_grad, own_grad] + gateds + [spread],
        flops=OUT_FLOPS,
        name="out_grad",
    )
    pieces = z.seq if z.direct else 1

    x_part, token = call(
        bind(own_x_grad_kernel, z),
        [struct(wide, F32), struct((16, PACK_LANES), F32)],
        [in_mats, own_grad, small],
        flops=OWN_X_FLOPS,
        name="own_x_grad",
    )

    def pack_after(after):
        packs = call(
            bind(pack_kernel, z),
            [struct((z.pack_rows // pieces, PACK_LANES))] * pieces,
            [tokens_t, got_grad, in_part, small, token, after],
            [pltpu.VMEM((z.pack_rows, PACK_LANES), BF16)],
            name="pack",
        )
        x_grad, done = call(
            bind(x_grad_kernel, z),
            [struct(wide), struct((16, PACK_LANES))],
            [in_mats, x_part, got_grad, packs[0]],
            flops=X_FLOPS,
            name="x_grad",
        )
        return packs, x_grad, done

    outs = [
        struct(chan_in.shape, F32),
        struct((z.blocks, z.blocks, z.block), F32),
        struct(seq_out.shape, F32),
    ]
    if z.direct:
        x_grad, first_rows, in_sum, out_sum, second_sum = sum_factors(
            z, core_sums, pack_after, own_grad, small, outs
        )
    else:
        packs, x_grad, _ = pack_after(small)
        first_rows, in_sum, out_sum, second_sum = sum_factors_plain(z, *first_parts, *packs, outs)
    return (x_grad[None], in_sum, jnp.transpose(out_sum, (2, 0, 1)), first_rows, second_sum)


def solution(mesh):
    in_specs = (P("dp", "seq", "chan"), P(), P(), P(), P(), P("dp", "seq", "chan"), P("dp", "seq"))
    out_specs = (P("dp", "seq", "chan"), P(), P(), P("seq", None), P())
    return jax.shard_map(
        per_device, mesh=mesh, in_specs=in_specs, out_specs=out_specs, check_vma=False
    )
```

time: 253 us -> 90.7 us (0.36)
  waiting for transfers between devices: 117 us -> 22 us
  blocking collectives: 41.9 us -> 0 us
  local copies, waits for them, and re-layouts: 35 us -> 6.4 us
  Pallas kernels: 0 us -> 26.6 us
  matrix products: 24.3 us -> 0 us
  starting transfers between devices: 16.5 us -> 34.3 us
  between operations: 14.3 us -> 0.96 us
  other arithmetic: 2.96 us -> 0 us
    psum x1 -> x0, waiting for transfers between devices: 93.8 us -> none  [per_device(): lax.psum((in_full, out_full, first_local, second_local), ('dp', 'chan', '...]
    psum x1 -> x0, blocking collectives: 41.9 us -> none  [per_device(): lax.psum((in_full, out_full, first_local, second_local), ('dp', 'chan', '...]
    ppermute x0 -> x38, starting transfers between devices: none -> 34.3 us  [swap(): return lax.ppermute(value, axis, [(i, i ^ step) for i in range(size)])]
    pallas_call x0 -> x30, Pallas kernels: none -> 26.6 us  [call(): pl.pallas_call(body, out_shape=tuple(outs), in_specs=[pl.BlockSpec(memory...]
    dot_general x12 -> x0, matrix products: 24.3 us -> none  [the longest x1 4.39 us: per_device(): jnp.einsum('stc,src->tr', channel_mix, returned_rows, preferred_element_t...]
    all_to_all x4 -> x0, waiting for transfers between devices: 23.2 us -> none  [the longest x1 14.1 us: per_device(): lax.all_to_all(first_mix, 'chan', split_axis=2, concat_axis=3, tiled=True)]
    ppermute x0 -> x38, waiting for transfers between devices: none -> 22 us  [swap(): return lax.ppermute(value, axis, [(i, i ^ step) for i in range(size)])]
    all_to_all x4 -> x0, starting transfers between devices: 16.2 us -> none  [the longest x1 4.33 us: per_device(): lax.all_to_all(first_grad, 'chan', split_axis=3, concat_axis=2, tiled=True)]
  transfers between devices with their start and end apart: 5 -> 38, of which waited for: 4 -> 18; matrix products, arithmetic and copies ran while one was open for 14% -> 3% of each run, Pallas kernels for 0% -> 27%
where the time goes in v2:
time: 90.7 us; the launch traced here: 90.3 us
  starting transfers between devices  34.3 us (38%)
  Pallas kernels  26.6 us (29%)
  waiting for transfers between devices  22 us (24%)
  local copies, waits for them, and re-layouts  6.4 us (7%)
  between operations  0.96 us (1%)
    ppermute x38, starting transfers between devices, swap(): return lax.ppermute(value, axis, [(i, i ^ step) for i in range(size)])  34.3 us
    pallas_call x30, Pallas kernels, call(): pl.pallas_call(body, out_shape=tuple(outs), in_specs=[pl.BlockSpec(memory...  26.6 us
    ppermute x38, waiting for transfers between devices, swap(): return lax.ppermute(value, axis, [(i, i ^ step) for i in range(size)])  22 us
    unnamed x20, local copies, waits for them, and re-layouts  4.11 us
    transpose x2, local copies, waits for them, and re-layouts, per_device(): jnp.transpose(factors, (1, 0, 2)).reshape(z.blocks * z.my_lanes, z.blocks)  2.29 us
  transfers between devices with their start and end apart: 38, of which 18 were waited for; matrix products, arithmetic and copies ran while one was open for 3% of the time, Pallas kernels for 27%

profile of v2, /device:TPU:0, one launch (start us, length us, event | category | flops | bytes accessed | tf_op | source)
XLA Modules:
  0.0 90.3 jit_solution(1888843501325014952)
XLA Ops:
  3.9 3.0 %collective-permute-start = (bf16[128,384]{1,0:T(8,128)(2,1)}, bf16[128,384]{1,0:T(8,128)(2,1)S(1)}, u32[]{:S(2)}, u32[]{:S(2)}) collective-permute-start(bf16[128,384]{1,0:T(8,128)(2,1)} %first_mix.5), channel_id=1, source_target_pairs={{0,4},{4,0},{1,5},{5,1},{2,6},{6,2},{3,7},{7,3},{8,12},{12,8},{9,1... | collective-permute-start | bytes 294920 | tf_op jit(solution)/shard_map/ppermute | solution.py:203
  9.2 2.0 %collective-permute-start.2 = (bf16[128,384]{1,0:T(8,128)(2,1)}, bf16[128,384]{1,0:T(8,128)(2,1)S(1)}, u32[]{:S(2)}, u32[]{:S(2)}) collective-permute-start(bf16[128,384]{1,0:T(8,128)(2,1)} %first_mix.7), channel_id=1, source_target_pairs={{0,4},{4,0},{1,5},{5,1},{2,6},{6,2},{3,7},{7,3},{8,12},{12,8},{9,1... | collective-permute-start | bytes 294920 | tf_op jit(solution)/shard_map/ppermute | solution.py:203
  13.1 1.6 %copy.12 = bf16[12,32,12]{2,1,0:T(8,128)(2,1)} copy(bf16[12,32,12]{1,2,0:T(8,128)(2,1)} %dynamic-slice_bitcast_fusion) | data formatting | bytes 18432 | tf_op jit(solution)/shard_map/transpose | solution.py:626
  16.7 2.3 %prepare.1 = (bf16[128,384]{1,0:T(8,128)(2,1)S(1)}, bf16[128,384]{1,0:T(8,128)(2,1)S(1)}, bf16[128,384]{1,0:T(8,128)(2,1)S(1)}, bf16[128,384]{1,0:T(8,128)(2,1)S...) custom-call(bf16[1024,384]{1,0:T(8,128)(2,1)S(1)} %bitcast.11, ...), custom_call_target="tpu_custom_call" | custom-call | flops 1 | bytes 1 | tf_op jit(solution)/shard_map/prepare/pallas_call | solution.py:47
  19.8 2.0 %collective-permute-start.4 = (bf16[2,64,384]{2,1,0:T(8,128)(2,1)S(1)}, bf16[2,64,384]{2,1,0:T(8,128)(2,1)S(1)}, u32[]{:S(2)}, u32[]{:S(2)}) collective-permute-start(bf16[2,64,384]{2,1,0:T(8,128)(2,1)S(1)} %get-tuple-element.99), channel_id=1, source_target_pairs={{0,2},{1,3},{2,0},{3,1},{4,6},{5,7},{6,4},{7,5},{8,10},{9,11},{10,... | collective-permute-start | bytes 294920 | tf_op jit(solution)/shard_map/ppermute | solution.py:203
  23.6 2.0 %collective-permute-start.6 = (bf16[2,64,384]{2,1,0:T(8,128)(2,1)S(1)}, bf16[2,64,384]{2,1,0:T(8,128)(2,1)S(1)}, u32[]{:S(2)}, u32[]{:S(2)}) collective-permute-start(bf16[2,64,384]{2,1,0:T(8,128)(2,1)S(1)} %get-tuple-element.101), channel_id=1, source_target_pairs={{0,2},{1,3},{2,0},{3,1},{4,6},{5,7},{6,4},{7,5},{8,10},{9,11},{10,... | collective-permute-start | bytes 294920 | tf_op jit(solution)/shard_map/ppermute | solution.py:203
  26.6 1.4 %row_mix.1 = (bf16[512,384]{1,0:T(8,128)(2,1)S(1)}, bf16[512,384]{1,0:T(8,128)(2,1)S(1)}, bf16[256,384]{1,0:T(8,128)(2,1)S(1)}, bf16[256,384]{1,0:T(8,128)(2,1)S(1)}, bf16[2,256,384]{2,1,0:T(8,128)(2,1)S(1)}) custom-call(bf16[1024,1024]{1,0:T(8,128)(2,1)S(1)} %get-tuple-element.82.turn_ref, bf16[256,384]{1,0:T(8,128)(2,1)S(1)} %get-tuple-element.86.rest_0_, ...), custom_call_target="tpu_custom_call" | custom-call | flops 1 | bytes 1 | tf_op jit(solution)/shard_map/row_mix/pallas_call | solution.py:47
  28.4 1.4 %collective-permute-done.6.refs_2_.rest_6_ = bf16[2,64,384]{2,1,0:T(8,128)(2,1)S(1)} collective-permute-done((bf16[2,64,384]{2,1,0:T(8,128)(2,1)S(1)}, bf16[2,64,384]{2,1,0:T(8,128)(2,1)S(1)}, u32[]{:S(2)}, u32[]{:S(2)}) %collective-permute-start.6) | collective-permute-done | bytes 98336 | tf_op jit(solution)/shard_map/ppermute | solution.py:203
  29.8 1.3 %collective-permute-done.7.refs_3_.rest_7_ = bf16[2,64,384]{2,1,0:T(8,128)(2,1)S(1)} collective-permute-done((bf16[2,64,384]{2,1,0:T(8,128)(2,1)S(1)}, bf16[2,64,384]{2,1,0:T(8,128)(2,1)S(1)}, u32[]{:S(2)}, u32[]{:S(2)}) %collective-permute-start.7) | collective-permute-done | bytes 98336 | tf_op jit(solution)/shard_map/ppermute | solution.py:203
  32.6 1.2 %seq_grad.1 = (bf16[1024,384]{1,0:T(8,128)(2,1)S(1)}, bf16[128,1024]{1,0:T(8,128)(2,1)S(1)}, bf16[128,1024]{1,0:T(8,128)(2,1)S(1)}, bf16[128,1024]{1,0:T(8,128)(2,1)S(1)}, bf16[128,1024]{1,0:T(8,128)(2,1)S(1)}) custom-call(bf16[512,384]{1,0:T(8,128)(2,1)S(1)} %get-tuple-element.93.mix0_ref, bf16[512,384]{1,0:T(8,128)(2,1)S(1)} %get-tuple-element.94.mix1_ref, ...), custom_call_target="tpu_custom_call" | custom-call | flops 1 | bytes 1 | tf_op jit(solution)/shard_map/seq_grad/pallas_call | solution.py:47
  36.9 1.7 %collective-permute-start.18 = (bf16[256,512]{1,0:T(8,128)(2,1)S(1)}, bf16[256,512]{1,0:T(8,128)(2,1)S(1)}, u32[]{:S(2)}, u32[]{:S(2)}) collective-permute-start(bf16[256,512]{1,0:T(8,128)(2,1)S(1)} %get-tuple-element.137), channel_id=1, source_target_pairs={{0,4},{4,0},{1,5},{5,1},{2,6},{6,2},{3,7},{7,3},{8,12},{12,8},{9,1... | collective-permute-start | bytes 786440 | tf_op jit(solution)/shard_map/ppermute | solution.py:203
  39.3 2.0 %seq_part.1 = (f32[1024,384]{1,0:T(8,128)S(1)}, f32[1024,384]{1,0:T(8,128)S(1)}) custom-call(bf16[1024,1024]{1,0:T(8,128)(2,1)S(1)} %copy-done.3, bf16[1024,384]{1,0:T(8,128)(2,1)S(1)} %get-tuple-element.108.all_ref.rows_ref, bf16[512,384]{1,0:T(8,128)(2,1)S(1)} %get-tuple-element.93.mix0_ref, bf16[512,384]{1,0:T(8,128)(2,1)S(1)} %get-tuple-element.94.mix1_ref, ...), custom_call_target="tpu_custom_call" | custom-call | flops 1 | bytes 1 | tf_op jit(solution)/shard_map/seq_part/pallas_call | solution.py:47
  41.8 1.4 %collective-permute-done.14.refs_0_.rest_1_ = bf16[2,256,384]{2,1,0:T(8,128)(2,1)S(1)} collective-permute-done((bf16[2,256,384]{2,1,0:T(8,128)(2,1)S(1)}, bf16[2,256,384]{2,1,0:T(8,128)(2,1)S(1)}, u32[]{:S(2)}, u32[]{:S(2)}) %collective-permute-start.14) | collective-permute-done | bytes 393248 | tf_op jit(solution)/shard_map/ppermute | solution.py:203
  43.3 1.4 %collective-permute-done.16.rest_3_ = bf16[256,384]{1,0:T(8,128)(2,1)S(1)} collective-permute-done((bf16[256,384]{1,0:T(8,128)(2,1)S(1)}, bf16[256,384]{1,0:T(8,128)(2,1)S(1)}, u32[]{:S(2)}, u32[]{:S(2)}) %collective-permute-start.16) | collective-permute-done | bytes 196640 | tf_op jit(solution)/shard_map/ppermute | solution.py:203
  44.7 2.0 %mix_grad.1 = (bf16[1024,384]{1,0:T(8,128)(2,1)S(1)}, bf16[512,384]{1,0:T(8,128)(2,1)S(1)}, bf16[512,384]{1,0:T(8,128)(2,1)S(1)}, bf16[1024,384]{1,0:T(8,128)(2,1)S(1)}) custom-call(f32[1024,384]{1,0:T(8,128)S(1)} %get-tuple-element.118.gate_ref, f32[1024,384]{1,0:T(8,128)S(1)} %get-tuple-element.119.rest_8_.part_ref, ...), custom_call_target="tpu_custom_call" | custom-call | flops 600000000 | bytes 1 | tf_op jit(solution)/shard_map/mix_grad/pallas_call | solution.py:47
  46.7 1.6 %collective-permute-done.19.got1_ref = bf16[256,512]{1,0:T(8,128)(2,1)S(1)} collective-permute-done((bf16[256,512]{1,0:T(8,128)(2,1)S(1)}, bf16[256,512]{1,0:T(8,128)(2,1)S(1)}, u32[]{:S(2)}, u32[]{:S(2)}) %collective-permute-start.19) | collective-permute-done | bytes 262176 | tf_op jit(solution)/shard_map/ppermute | solution.py:203
  49.2 1.5 %collective-permute-start.21 = (bf16[128,512]{1,0:T(8,128)(2,1)S(1)}, bf16[128,512]{1,0:T(8,128)(2,1)S(1)}, u32[]{:S(2)}, u32[]{:S(2)}) collective-permute-start(bf16[128,512]{1,0:T(8,128)(2,1)S(1)} %get-tuple-element.142), channel_id=1, source_target_pairs={{0,4},{4,0},{1,5},{5,1},{2,6},{6,2},{3,7},{7,3},{8,12},{12,8},{9,1... | collective-permute-start | bytes 393224 | tf_op jit(solution)/shard_map/ppermute | solution.py:203
  51.2 3.5 %out_grad.1 = (f32[192,128]{1,0:T(8,128)S(1)}, bf16[64,128]{1,0:T(8,128)(2,1)S(1)}) custom-call(bf16[384,512]{1,0:T(8,128)(2,1)S(1)} %get-tuple-element.124.rest_0_, bf16[384,512]{1,0:T(8,128)(2,1)S(1)} %get-tuple-element.125.rest_1_, bf16[384,1024]{1,0:T(8,128)(2,1)S(1)} %get-tuple-element.122.refs_1_.rest_2_.xt_ref, ...), custom_call_target="tpu_custom_call" | custom-call | flops 1 | bytes 1 | tf_op jit(solution)/shard_map/out_grad/pallas_call | solution.py:47
  55.7 1.6 %collective-permute-start.22 = (bf16[256,128]{1,0:T(8,128)(2,1)S(1)}, bf16[256,128]{1,0:T(8,128)(2,1)S(1)}, u32[]{:S(2)}, u32[]{:S(2)}) collective-permute-start(bf16[256,128]{1,0:T(8,128)(2,1)S(1)} %get-tuple-element.146), channel_id=1, source_target_pairs={{0,8},{8,0},{16,24},{24,16},{1,9},{9,1},{17,25},{25,17},{2,10},{10... | collective-permute-start | bytes 196616 | tf_op jit(solution)/shard_map/ppermute | solution.py:203
  57.3 2.6 %collective-permute-start.23 = (bf16[256,128]{1,0:T(8,128)(2,1)S(1)}, bf16[256,128]{1,0:T(8,128)(2,1)S(1)}, u32[]{:S(2)}, u32[]{:S(2)}) collective-permute-start(bf16[256,128]{1,0:T(8,128)(2,1)S(1)} %get-tuple-element.147), channel_id=1, source_target_pairs={{0,16},{8,24},{16,0},{24,8},{1,17},{9,25},{17,1},{25,9},{2,18},{10... | collective-permute-start | bytes 196616 | tf_op jit(solution)/shard_map/ppermute | solution.py:203
  60.8 1.6 %collective-permute-done.17.got_ref = bf16[512,384]{1,0:T(8,128)(2,1)S(1)} collective-permute-done((bf16[512,384]{1,0:T(8,128)(2,1)S(1)}, bf16[512,384]{1,0:T(8,128)(2,1)S(1)}, u32[]{:S(2)}, u32[]{:S(2)}) %collective-permute-start.17) | collective-permute-done | bytes 393248 | tf_op jit(solution)/shard_map/ppermute | solution.py:203
  63.2 1.4 %collective-permute-start.26 = (bf16[64,128]{1,0:T(8,128)(2,1)S(1)}, bf16[64,128]{1,0:T(8,128)(2,1)S(1)}, u32[]{:S(2)}, u32[]{:S(2)}) collective-permute-start(bf16[64,128]{1,0:T(8,128)(2,1)S(1)} %get-tuple-element.150), channel_id=1, source_target_pairs={{0,2},{1,3},{2,0},{3,1},{4,6},{5,7},{6,4},{7,5},{8,10},{9,11},{10,... | collective-permute-start | bytes 49160 | tf_op jit(solution)/shard_map/ppermute | solution.py:203
  65.5 1.5 %collective-permute-done.26.c_ref = bf16[64,128]{1,0:T(8,128)(2,1)S(1)} collective-permute-done((bf16[64,128]{1,0:T(8,128)(2,1)S(1)}, bf16[64,128]{1,0:T(8,128)(2,1)S(1)}, u32[]{:S(2)}, u32[]{:S(2)}) %collective-permute-start.26) | collective-permute-done | bytes 16416 | tf_op jit(solution)/shard_map/ppermute | solution.py:203
  67.9 3.7 %collective-permute-start.30 = (bf16[320,128]{1,0:T(8,128)(2,1)S(1)}, bf16[320,128]{1,0:T(8,128)(2,1)S(1)}, u32[]{:S(2)}, u32[]{:S(2)}) collective-permute-start(bf16[320,128]{1,0:T(8,128)(2,1)S(1)} %z_sum.1.refs_0_), channel_id=1, source_target_pairs={{0,24},{8,16},{16,8},{24,0},{1,25},{9,17},{17,9},{25,1},{2,26},{10... | collective-permute-start | bytes 245768 | tf_op jit(solution)/shard_map/ppermute | solution.py:203
  72.3 1.6 %x_grad.1 = (bf16[1024,384]{1,0:T(8,128)(2,1)}, bf16[16,128]{1,0:T(8,128)(2,1)S(1)}) custom-call(bf16[4,384,384]{2,1,0:T(8,128)(2,1)S(1)} %get-tuple-element.81.win_ref, f32[1024,384]{1,0:T(8,128)S(1)} %get-tuple-element.133.part_ref, bf16[512,384]{1,0:T(8,128)(2,1)S(1)} %collective-permute-done.17.got_ref, ...), custom_call_target="tpu_custom_call" | custom-call | flops 1 | bytes 1 | tf_op jit(solution)/shard_map/x_grad/pallas_call | solution.py:47
  73.9 1.6 %collective-permute-start.31 = (bf16[320,128]{1,0:T(8,128)(2,1)S(1)}, bf16[320,128]{1,0:T(8,128)(2,1)S(1)}, u32[]{:S(2)}, u32[]{:S(2)}) collective-permute-start(bf16[320,128]{1,0:T(8,128)(2,1)S(1)} %z_sum.1.refs_0_), channel_id=1, source_target_pairs={{0,4},{4,0},{1,5},{5,1},{2,6},{6,2},{3,7},{7,3},{8,12},{12,8},{9,1... | collective-permute-start | bytes 245768 | tf_op jit(solution)/shard_map/ppermute | solution.py:203
  76.5 2.3 %collective-permute-done.29.refs_2_ = bf16[320,128]{1,0:T(8,128)(2,1)S(1)} collective-permute-done((bf16[320,128]{1,0:T(8,128)(2,1)S(1)}, bf16[320,128]{1,0:T(8,128)(2,1)S(1)}, u32[]{:S(2)}, u32[]{:S(2)}) %collective-permute-start.29) | collective-permute-done | bytes 81952 | tf_op jit(solution)/shard_map/ppermute | solution.py:203
  78.8 1.5 %collective-permute-start.33 = (bf16[320,128]{1,0:T(8,128)(2,1)S(1)}, bf16[320,128]{1,0:T(8,128)(2,1)S(1)}, u32[]{:S(2)}, u32[]{:S(2)}) collective-permute-start(bf16[320,128]{1,0:T(8,128)(2,1)S(1)} %collective-permute-done.29.refs_2_), channel_id=1, source_target_pairs={{0,4},{4,0},{1,5},{5,1},{2,6},{6,2},{3,7},{7,3},{8,12},{12,8},{9,1... | collective-permute-start | bytes 245768 | tf_op jit(solution)/shard_map/ppermute | solution.py:203
  80.8 2.9 %collective-permute-done.33.refs_6_ = bf16[320,128]{1,0:T(8,128)(2,1)S(1)} collective-permute-done((bf16[320,128]{1,0:T(8,128)(2,1)S(1)}, bf16[320,128]{1,0:T(8,128)(2,1)S(1)}, u32[]{:S(2)}, u32[]{:S(2)}) %collective-permute-start.33) | collective-permute-done | bytes 81952 | tf_op jit(solution)/shard_map/ppermute | solution.py:203
  84.9 1.2 %collective-permute-start.36 = (bf16[128,128]{1,0:T(8,128)(2,1)S(1)}, bf16[128,128]{1,0:T(8,128)(2,1)S(1)}, u32[]{:S(2)}, u32[]{:S(2)}) collective-permute-start(bf16[128,128]{1,0:T(8,128)(2,1)S(1)} %line_sum.1.refs_8_), channel_id=1, source_target_pairs={{0,2},{1,3},{2,0},{3,1},{4,6},{5,7},{6,4},{7,5},{8,10},{9,11},{10,... | collective-permute-start | bytes 98312 | tf_op jit(solution)/shard_map/ppermute | solution.py:203
  86.7 1.5 %collective-permute-done.37.refs_11_ = bf16[128,128]{1,0:T(8,128)(2,1)S(1)} collective-permute-done((bf16[128,128]{1,0:T(8,128)(2,1)S(1)}, bf16[128,128]{1,0:T(8,128)(2,1)S(1)}, u32[]{:S(2)}, u32[]{:S(2)}) %collective-permute-start.37) | collective-permute-done | bytes 32800 | tf_op jit(solution)/shard_map/ppermute | solution.py:203
  89.0 1.3 %last.1 = (f32[256,1024]{1,0:T(8,128)}, f32[12,64,64]{2,1,0:T(8,128)}, f32[12,12,64]{2,1,0:T(8,128)}, f32[4,4]{1,0:T(4,128)}) custom-call(bf16[320,128]{1,0:T(8,128)(2,1)S(1)} %z_sum.1.refs_0_, bf16[320,128]{1,0:T(8,128)(2,1)S(1)} %collective-permute-done.28.refs_1_, bf16[320,128]{1,0:T(8,128)(2,1)S(1)} %collective-permute-done.29.refs_2_, ...), custom_call_target="tpu_custom_call" | custom-call | flops 1 | bytes 1 | tf_op jit(solution)/shard_map/last/pallas_call | solution.py:47
  (96 shorter events, 29.8 us)
Async XLA Ops:
  3.9 15.2 %collective-permute-start = (bf16[128,384]{1,0:T(8,128)(2,1)}, bf16[128,384]{1,0:T(8,128)(2,1)S(1)}, u32[]{:S(2)}, u32[]{:S(2)}) collective-permute-start(bf16[128,384]{1,0:T(8,128)(2,1)} %first_mix.5), channel_id=1, source_target_pairs={{0,4},{4,0},{1,5},{5,1},{2,6},{6,2},{3,7},{7,3},{8,12},{12,8},{9,1... | collective-permute-start | bytes 294920 | tf_op jit(solution)/shard_map/ppermute | solution.py:203
  8.1 13.8 %collective-permute-start.1 = (bf16[128,384]{1,0:T(8,128)(2,1)}, bf16[128,384]{1,0:T(8,128)(2,1)S(1)}, u32[]{:S(2)}, u32[]{:S(2)}) collective-permute-start(bf16[128,384]{1,0:T(8,128)(2,1)} %first_mix.6), channel_id=1, source_target_pairs={{0,4},{4,0},{1,5},{5,1},{2,6},{6,2},{3,7},{7,3},{8,12},{12,8},{9,1... | collective-permute-start | bytes 294920 | tf_op jit(solution)/shard_map/ppermute | solution.py:203
  9.2 13.6 %collective-permute-start.2 = (bf16[128,384]{1,0:T(8,128)(2,1)}, bf16[128,384]{1,0:T(8,128)(2,1)S(1)}, u32[]{:S(2)}, u32[]{:S(2)}) collective-permute-start(bf16[128,384]{1,0:T(8,128)(2,1)} %first_mix.7), channel_id=1, source_target_pairs={{0,4},{4,0},{1,5},{5,1},{2,6},{6,2},{3,7},{7,3},{8,12},{12,8},{9,1... | collective-permute-start | bytes 294920 | tf_op jit(solution)/shard_map/ppermute | solution.py:203
  12.4 13.2 %collective-permute-start.3 = (bf16[128,384]{1,0:T(8,128)(2,1)}, bf16[128,384]{1,0:T(8,128)(2,1)S(1)}, u32[]{:S(2)}, u32[]{:S(2)}) collective-permute-start(bf16[128,384]{1,0:T(8,128)(2,1)} %first_mix.4.after_ref), channel_id=1, source_target_pairs={{0,4},{4,0},{1,5},{5,1},{2,6},{6,2},{3,7},{7,3},{8,12},{12,8},{9,1... | collective-permute-start | bytes 294920 | tf_op jit(solution)/shard_map/ppermute | solution.py:203
  19.8 8.1 %collective-permute-start.4 = (bf16[2,64,384]{2,1,0:T(8,128)(2,1)S(1)}, bf16[2,64,384]{2,1,0:T(8,128)(2,1)S(1)}, u32[]{:S(2)}, u32[]{:S(2)}) collective-permute-start(bf16[2,64,384]{2,1,0:T(8,128)(2,1)S(1)} %get-tuple-element.99), channel_id=1, source_target_pairs={{0,2},{1,3},{2,0},{3,1},{4,6},{5,7},{6,4},{7,5},{8,10},{9,11},{10,... | collective-permute-start | bytes 294920 | tf_op jit(solution)/shard_map/ppermute | solution.py:203
  22.7 5.8 %collective-permute-start.5 = (bf16[2,64,384]{2,1,0:T(8,128)(2,1)S(1)}, bf16[2,64,384]{2,1,0:T(8,128)(2,1)S(1)}, u32[]{:S(2)}, u32[]{:S(2)}) collective-permute-start(bf16[2,64,384]{2,1,0:T(8,128)(2,1)S(1)} %get-tuple-element.100), channel_id=1, source_target_pairs={{0,2},{1,3},{2,0},{3,1},{4,6},{5,7},{6,4},{7,5},{8,10},{9,11},{10,... | collective-permute-start | bytes 294920 | tf_op jit(solution)/shard_map/ppermute | solution.py:203
  23.6 6.2 %collective-permute-start.6 = (bf16[2,64,384]{2,1,0:T(8,128)(2,1)S(1)}, bf16[2,64,384]{2,1,0:T(8,128)(2,1)S(1)}, u32[]{:S(2)}, u32[]{:S(2)}) collective-permute-start(bf16[2,64,384]{2,1,0:T(8,128)(2,1)S(1)} %get-tuple-element.101), channel_id=1, source_target_pairs={{0,2},{1,3},{2,0},{3,1},{4,6},{5,7},{6,4},{7,5},{8,10},{9,11},{10,... | collective-permute-start | bytes 294920 | tf_op jit(solution)/shard_map/ppermute | solution.py:203
  26.4 4.7 %collective-permute-start.7 = (bf16[2,64,384]{2,1,0:T(8,128)(2,1)S(1)}, bf16[2,64,384]{2,1,0:T(8,128)(2,1)S(1)}, u32[]{:S(2)}, u32[]{:S(2)}) collective-permute-start(bf16[2,64,384]{2,1,0:T(8,128)(2,1)S(1)} %get-tuple-element.102), channel_id=1, source_target_pairs={{0,2},{1,3},{2,0},{3,1},{4,6},{5,7},{6,4},{7,5},{8,10},{9,11},{10,... | collective-permute-start | bytes 294920 | tf_op jit(solution)/shard_map/ppermute | solution.py:203
  26.5 5.4 %collective-permute-start.8 = (bf16[256,384]{1,0:T(8,128)(2,1)S(1)}, bf16[256,384]{1,0:T(8,128)(2,1)S(1)}, u32[]{:S(2)}, u32[]{:S(2)}) collective-permute-start(bf16[256,384]{1,0:T(8,128)(2,1)S(1)} %own_mate.1), channel_id=1, source_target_pairs={{0,1},{1,0},{2,3},{3,2},{4,5},{5,4},{6,7},{7,6},{8,9},{9,8},{10,11... | collective-permute-start | bytes 589832 | tf_op jit(solution)/shard_map/ppermute | solution.py:203
  31.2 12.0 %collective-permute-start.14 = (bf16[2,256,384]{2,1,0:T(8,128)(2,1)S(1)}, bf16[2,256,384]{2,1,0:T(8,128)(2,1)S(1)}, u32[]{:S(2)}, u32[]{:S(2)}) collective-permute-start(bf16[2,256,384]{2,1,0:T(8,128)(2,1)S(1)} %get-tuple-element.120), channel_id=1, source_target_pairs={{0,2},{1,3},{2,0},{3,1},{4,6},{5,7},{6,4},{7,5},{8,10},{9,11},{10,... | collective-permute-start | bytes 1179656 | tf_op jit(solution)/shard_map/ppermute | solution.py:203
  33.8 2.2 %collective-permute-start.10 = (bf16[128,1024]{1,0:T(8,128)(2,1)S(1)}, bf16[128,1024]{1,0:T(8,128)(2,1)S(1)}, u32[]{:S(2)}, u32[]{:S(2)}) collective-permute-start(bf16[128,1024]{1,0:T(8,128)(2,1)S(1)} %get-tuple-element.113), channel_id=1, source_target_pairs={{0,1},{1,0},{2,3},{3,2},{4,5},{5,4},{6,7},{7,6},{8,9},{9,8},{10,11... | collective-permute-start | bytes 786440 | tf_op jit(solution)/shard_map/ppermute | solution.py:203
  36.9 9.7 %collective-permute-start.18 = (bf16[256,512]{1,0:T(8,128)(2,1)S(1)}, bf16[256,512]{1,0:T(8,128)(2,1)S(1)}, u32[]{:S(2)}, u32[]{:S(2)}) collective-permute-start(bf16[256,512]{1,0:T(8,128)(2,1)S(1)} %get-tuple-element.137), channel_id=1, source_target_pairs={{0,4},{4,0},{1,5},{5,1},{2,6},{6,2},{3,7},{7,3},{8,12},{12,8},{9,1... | collective-permute-start | bytes 786440 | tf_op jit(solution)/shard_map/ppermute | solution.py:203
  38.6 9.7 %collective-permute-start.19 = (bf16[256,512]{1,0:T(8,128)(2,1)S(1)}, bf16[256,512]{1,0:T(8,128)(2,1)S(1)}, u32[]{:S(2)}, u32[]{:S(2)}) collective-permute-start(bf16[256,512]{1,0:T(8,128)(2,1)S(1)} %get-tuple-element.139), channel_id=1, source_target_pairs={{0,2},{1,3},{2,0},{3,1},{4,6},{5,7},{6,4},{7,5},{8,10},{9,11},{10,... | collective-permute-start | bytes 786440 | tf_op jit(solution)/shard_map/ppermute | solution.py:203
  39.3 4.0 %collective-permute-start.15 = (bf16[256,384]{1,0:T(8,128)(2,1)S(1)}, bf16[256,384]{1,0:T(8,128)(2,1)S(1)}, u32[]{:S(2)}, u32[]{:S(2)}) collective-permute-start(bf16[256,384]{1,0:T(8,128)(2,1)S(1)} %get-tuple-element.121), channel_id=1, source_target_pairs={{0,1},{1,0},{2,3},{3,2},{4,5},{5,4},{6,7},{7,6},{8,9},{9,8},{10,11... | collective-permute-start | bytes 589832 | tf_op jit(solution)/shard_map/ppermute | solution.py:203
  48.4 6.3 %collective-permute-start.20 = (bf16[128,512]{1,0:T(8,128)(2,1)S(1)}, bf16[128,512]{1,0:T(8,128)(2,1)S(1)}, u32[]{:S(2)}, u32[]{:S(2)}) collective-permute-start(bf16[128,512]{1,0:T(8,128)(2,1)S(1)} %get-tuple-element.141), channel_id=1, source_target_pairs={{0,2},{1,3},{2,0},{3,1},{4,6},{5,7},{6,4},{7,5},{8,10},{9,11},{10,... | collective-permute-start | bytes 393224 | tf_op jit(solution)/shard_map/ppermute | solution.py:203
  49.2 6.4 %collective-permute-start.21 = (bf16[128,512]{1,0:T(8,128)(2,1)S(1)}, bf16[128,512]{1,0:T(8,128)(2,1)S(1)}, u32[]{:S(2)}, u32[]{:S(2)}) collective-permute-start(bf16[128,512]{1,0:T(8,128)(2,1)S(1)} %get-tuple-element.142), channel_id=1, source_target_pairs={{0,4},{4,0},{1,5},{5,1},{2,6},{6,2},{3,7},{7,3},{8,12},{12,8},{9,1... | collective-permute-start | bytes 393224 | tf_op jit(solution)/shard_map/ppermute | solution.py:203
  50.7 11.7 %collective-permute-start.17 = (bf16[512,384]{1,0:T(8,128)(2,1)S(1)}, bf16[512,384]{1,0:T(8,128)(2,1)S(1)}, u32[]{:S(2)}, u32[]{:S(2)}) collective-permute-start(bf16[512,384]{1,0:T(8,128)(2,1)S(1)} %get-tuple-element.134), channel_id=1, source_target_pairs={{0,4},{4,0},{1,5},{5,1},{2,6},{6,2},{3,7},{7,3},{8,12},{12,8},{9,1... | collective-permute-start | bytes 1179656 | tf_op jit(solution)/shard_map/ppermute | solution.py:203
  55.7 12.1 %collective-permute-start.22 = (bf16[256,128]{1,0:T(8,128)(2,1)S(1)}, bf16[256,128]{1,0:T(8,128)(2,1)S(1)}, u32[]{:S(2)}, u32[]{:S(2)}) collective-permute-start(bf16[256,128]{1,0:T(8,128)(2,1)S(1)} %get-tuple-element.146), channel_id=1, source_target_pairs={{0,8},{8,0},{16,24},{24,16},{1,9},{9,1},{17,25},{25,17},{2,10},{10... | collective-permute-start | bytes 196616 | tf_op jit(solution)/shard_map/ppermute | solution.py:203
  57.3 10.5 %collective-permute-start.23 = (bf16[256,128]{1,0:T(8,128)(2,1)S(1)}, bf16[256,128]{1,0:T(8,128)(2,1)S(1)}, u32[]{:S(2)}, u32[]{:S(2)}) collective-permute-start(bf16[256,128]{1,0:T(8,128)(2,1)S(1)} %get-tuple-element.147), channel_id=1, source_target_pairs={{0,16},{8,24},{16,0},{24,8},{1,17},{9,25},{17,1},{25,9},{2,18},{10... | collective-permute-start | bytes 196616 | tf_op jit(solution)/shard_map/ppermute | solution.py:203
  59.9 7.9 %collective-permute-start.24 = (bf16[256,128]{1,0:T(8,128)(2,1)S(1)}, bf16[256,128]{1,0:T(8,128)(2,1)S(1)}, u32[]{:S(2)}, u32[]{:S(2)}) collective-permute-start(bf16[256,128]{1,0:T(8,128)(2,1)S(1)} %get-tuple-element.148), channel_id=1, source_target_pairs={{0,24},{8,16},{16,8},{24,0},{1,25},{9,17},{17,9},{25,1},{2,26},{10... | collective-permute-start | bytes 196616 | tf_op jit(solution)/shard_map/ppermute | solution.py:203
  63.2 3.8 %collective-permute-start.26 = (bf16[64,128]{1,0:T(8,128)(2,1)S(1)}, bf16[64,128]{1,0:T(8,128)(2,1)S(1)}, u32[]{:S(2)}, u32[]{:S(2)}) collective-permute-start(bf16[64,128]{1,0:T(8,128)(2,1)S(1)} %get-tuple-element.150), channel_id=1, source_target_pairs={{0,2},{1,3},{2,0},{3,1},{4,6},{5,7},{6,4},{7,5},{8,10},{9,11},{10,... | collective-permute-start | bytes 49160 | tf_op jit(solution)/shard_map/ppermute | solution.py:203
  64.6 3.2 %collective-permute-start.27 = (bf16[64,128]{1,0:T(8,128)(2,1)S(1)}, bf16[64,128]{1,0:T(8,128)(2,1)S(1)}, u32[]{:S(2)}, u32[]{:S(2)}) collective-permute-start(bf16[64,128]{1,0:T(8,128)(2,1)S(1)} %get-tuple-element.151), channel_id=1, source_target_pairs={{0,3},{1,2},{2,1},{3,0},{4,7},{5,6},{6,5},{7,4},{8,11},{9,10},{10,... | collective-permute-start | bytes 49160 | tf_op jit(solution)/shard_map/ppermute | solution.py:203
  67.9 7.7 %collective-permute-start.30 = (bf16[320,128]{1,0:T(8,128)(2,1)S(1)}, bf16[320,128]{1,0:T(8,128)(2,1)S(1)}, u32[]{:S(2)}, u32[]{:S(2)}) collective-permute-start(bf16[320,128]{1,0:T(8,128)(2,1)S(1)} %z_sum.1.refs_0_), channel_id=1, source_target_pairs={{0,24},{8,16},{16,8},{24,0},{1,25},{9,17},{17,9},{25,1},{2,26},{10... | collective-permute-start | bytes 245768 | tf_op jit(solution)/shard_map/ppermute | solution.py:203
  71.6 7.2 %collective-permute-start.29 = (bf16[320,128]{1,0:T(8,128)(2,1)S(1)}, bf16[320,128]{1,0:T(8,128)(2,1)S(1)}, u32[]{:S(2)}, u32[]{:S(2)}) collective-permute-start(bf16[320,128]{1,0:T(8,128)(2,1)S(1)} %z_sum.1.refs_0_), channel_id=1, source_target_pairs={{0,16},{8,24},{16,0},{24,8},{1,17},{9,25},{17,1},{25,9},{2,18},{10... | collective-permute-start | bytes 245768 | tf_op jit(solution)/shard_map/ppermute | solution.py:203
  71.6 8.7 %collective-permute-start.28 = (bf16[320,128]{1,0:T(8,128)(2,1)S(1)}, bf16[320,128]{1,0:T(8,128)(2,1)S(1)}, u32[]{:S(2)}, u32[]{:S(2)}) collective-permute-start(bf16[320,128]{1,0:T(8,128)(2,1)S(1)} %z_sum.1.refs_0_), channel_id=1, source_target_pairs={{0,8},{8,0},{16,24},{24,16},{1,9},{9,1},{17,25},{25,17},{2,10},{10... | collective-permute-start | bytes 245768 | tf_op jit(solution)/shard_map/ppermute | solution.py:203
  73.9 6.9 %collective-permute-start.31 = (bf16[320,128]{1,0:T(8,128)(2,1)S(1)}, bf16[320,128]{1,0:T(8,128)(2,1)S(1)}, u32[]{:S(2)}, u32[]{:S(2)}) collective-permute-start(bf16[320,128]{1,0:T(8,128)(2,1)S(1)} %z_sum.1.refs_0_), channel_id=1, source_target_pairs={{0,4},{4,0},{1,5},{5,1},{2,6},{6,2},{3,7},{7,3},{8,12},{12,8},{9,1... | collective-permute-start | bytes 245768 | tf_op jit(solution)/shard_map/ppermute | solution.py:203
  75.5 5.3 %collective-permute-start.34 = (bf16[320,128]{1,0:T(8,128)(2,1)S(1)}, bf16[320,128]{1,0:T(8,128)(2,1)S(1)}, u32[]{:S(2)}, u32[]{:S(2)}) collective-permute-start(bf16[320,128]{1,0:T(8,128)(2,1)S(1)} %pass_on.1), channel_id=1, source_target_pairs={{0,4},{4,0},{1,5},{5,1},{2,6},{6,2},{3,7},{7,3},{8,12},{12,8},{9,1... | collective-permute-start | bytes 245768 | tf_op jit(solution)/shard_map/ppermute | solution.py:203
  78.8 4.9 %collective-permute-start.33 = (bf16[320,128]{1,0:T(8,128)(2,1)S(1)}, bf16[320,128]{1,0:T(8,128)(2,1)S(1)}, u32[]{:S(2)}, u32[]{:S(2)}) collective-permute-start(bf16[320,128]{1,0:T(8,128)(2,1)S(1)} %collective-permute-done.29.refs_2_), channel_id=1, source_target_pairs={{0,4},{4,0},{1,5},{5,1},{2,6},{6,2},{3,7},{7,3},{8,12},{12,8},{9,1... | collective-permute-start | bytes 245768 | tf_op jit(solution)/shard_map/ppermute | solution.py:203
  80.3 4.4 %collective-permute-start.32 = (bf16[320,128]{1,0:T(8,128)(2,1)S(1)}, bf16[320,128]{1,0:T(8,128)(2,1)S(1)}, u32[]{:S(2)}, u32[]{:S(2)}) collective-permute-start(bf16[320,128]{1,0:T(8,128)(2,1)S(1)} %collective-permute-done.28.refs_1_), channel_id=1, source_target_pairs={{0,4},{4,0},{1,5},{5,1},{2,6},{6,2},{3,7},{7,3},{8,12},{12,8},{9,1... | collective-permute-start | bytes 245768 | tf_op jit(solution)/shard_map/ppermute | solution.py:203
  84.8 3.4 %collective-permute-start.37 = (bf16[128,128]{1,0:T(8,128)(2,1)S(1)}, bf16[128,128]{1,0:T(8,128)(2,1)S(1)}, u32[]{:S(2)}, u32[]{:S(2)}) collective-permute-start(bf16[128,128]{1,0:T(8,128)(2,1)S(1)} %line_sum.1.refs_8_), channel_id=1, source_target_pairs={{0,3},{1,2},{2,1},{3,0},{4,7},{5,6},{6,5},{7,4},{8,11},{9,10},{10,... | collective-permute-start | bytes 98312 | tf_op jit(solution)/shard_map/ppermute | solution.py:203
  84.9 4.2 %collective-permute-start.36 = (bf16[128,128]{1,0:T(8,128)(2,1)S(1)}, bf16[128,128]{1,0:T(8,128)(2,1)S(1)}, u32[]{:S(2)}, u32[]{:S(2)}) collective-permute-start(bf16[128,128]{1,0:T(8,128)(2,1)S(1)} %line_sum.1.refs_8_), channel_id=1, source_target_pairs={{0,2},{1,3},{2,0},{3,1},{4,6},{5,7},{6,4},{7,5},{8,10},{9,11},{10,... | collective-permute-start | bytes 98312 | tf_op jit(solution)/shard_map/ppermute | solution.py:203
  86.0 3.0 %collective-permute-start.35 = (bf16[128,128]{1,0:T(8,128)(2,1)S(1)}, bf16[128,128]{1,0:T(8,128)(2,1)S(1)}, u32[]{:S(2)}, u32[]{:S(2)}) collective-permute-start(bf16[128,128]{1,0:T(8,128)(2,1)S(1)} %line_sum.1.refs_8_), channel_id=1, source_target_pairs={{0,1},{1,0},{2,3},{3,2},{4,5},{5,4},{6,7},{7,6},{8,9},{9,8},{10,11... | collective-permute-start | bytes 98312 | tf_op jit(solution)/shard_map/ppermute | solution.py:203
  (16 other events, 71.7 us)
